TPU v7x, 32 devices: a whole 2x2x4 slice. The times are simulated.
32 devices in a mesh: groups: 2 (over y), tm: 4 (over z), space: 4 (over x, core).
Axes of the slice: x: 2, y: 2, z: 4, core: 2. Of those that a mesh axis runs over, the one named last changes fastest.
Arguments:
- frames_in: bfloat16 [64, 112896], P(('groups', 'tm'), 'space'), parts along dimension 0, may hold values from -6 to 6
- arrive_len: int32 [8], P('groups'), parts along dimension 0, may hold values from 1 to 8, 16 in all
- clip_len: int32 [8], P('groups'), parts along dimension 0, may hold values from 1 to 8, 16 in all
- tile_pick: int32 [392, 196], P('groups'), parts along dimension 0, may hold values from 0 to 1, as said below
- norm_gain: float32 [576], replicated, may hold values from 0.5 to 1.5
- in_weight: bfloat16 [2, 576, 1152], replicated, may hold values from -0.25 to 0.25
- proj_weight: bfloat16 [4, 1152, 68], P(None, 'space'), may hold values from -0.1875 to 0.1875
- dt_weight: bfloat16 [4, 36, 1152], P(None, None, 'space'), may hold values from -1 to 1
- dt_bias: float32 [4, 1152], P(None, 'space'), may hold values from -4 to -1
- decay_rate: float32 [4, 1152, 16], P(None, 'space'), may hold values from 0.05 to 4
- skip_gain: float32 [4, 1152], P(None, 'space'), may hold values from 0.5 to 1.5
- out_weight: bfloat16 [1152, 576], P('space'), may hold values from -0.1875 to 0.1875
Outputs:
- mixed: bfloat16 [196, 18432], P('tm', ('groups', 'space')), parts along dimension 1
There are 2 independent parts, one for each index of `groups`. A program takes and returns all parts, laid end to end along the dimension named above; an argument that names none is the same for every part. Nothing has to cross between parts.
Inputs may be any that keep to these rules, and one draw needn't show every extreme that they name: Device j of tm holds in its first arrive_len[j] slots the blocks of the packed sequence that follow those of devices before it; its other slots are padding. `clip_len`: the clips cover the 16 frames end to end. `tile_pick`: each patch has exactly one 1 in its row; each column holds at most one 1; the 49 columns of each device of tm are used from its first one on, 49 or 48 of them.
All inputs are finite; a program needn't handle non-finite values.
Results may differ from a plain program's by a relative error of at most 0.015.
Values may be sent and summed in bfloat16 or wider, within the bound.
A program may use at most 64 MiB of HBM per device.

v0:
```python
import functools

import jax
import jax.numpy as jnp
import numpy as np
from jax import lax
from jax.experimental import pallas as pl
from jax.experimental.pallas import tpu as pltpu
from jax.sharding import PartitionSpec as P

PATCHES = 196
OWN_BLK = 4
IN_BLK = 8
ROWS = 4
STATE = 16
RANK = 36
HALF = 2 * (RANK + 2 * STATE)
EPSILON = 1e-05
LOG2E = 1.4426950408889634
CLOSED = 1e4
F32 = jnp.float32
BF16 = jnp.bfloat16


def chunks_of(part):
    assert 0 < part % 128 <= 32
    return tuple((512 * i, 512) for i in range(part // 128)) + ((512 * (part // 128), 128),)


def lanes_of(part):
    return 512 * (part // 128) + 128


def constants():
    perm = np.zeros((512, 512), np.float32)
    for r in range(ROWS):
        for ch in range(128):
            perm[r * 128 + ch, (ch // 32) * 128 + r * 32 + ch % 32] = 1
    spread = np.zeros((ROWS * STATE, STATE * 128), np.float32)
    for r in range(ROWS):
        for s in range(STATE):
            spread[r * STATE + s, s * 128 + r * 32 : s * 128 + r * 32 + 32] = 1
    return perm, spread


def widening(part):
    widen = np.zeros((part, lanes_of(part)), np.float32)
    for ch in range(part):
        for r in range(ROWS):
            widen[ch, (ch // 32) * 128 + r * 32 + ch % 32] = 1
    return widen


PERM, SPREAD = constants()


def dot(a, b):
    return jnp.dot(a, b, preferred_element_type=F32)


def pack_rows(wide, tail, perm_ref, chunk, size):
    wide = wide if size == 512 else None
    if wide is not None:
        return dot(jnp.concatenate([wide(r, chunk) for r in range(ROWS)], axis=1), perm_ref[...])
    total = 0.0
    for r in range(ROWS):
        piece = tail(r)
        total = total + dot(piece, perm_ref[128 * r : 128 * r + piece.shape[1], 0:128])
    return total


def store_tiles(ref, k, start, block):
    rows = ref.shape[1]
    flat = ref.reshape(2, rows * STATE, 128)
    for t in range(block.shape[1] // 128):
        flat[k, pl.ds(start // 128 + t, rows, stride=STATE), :] = block[:, 128 * t : 128 * t + 128]


def load_tiles(ref, k, start, size):
    rows = ref.shape[1]
    flat = ref.reshape(2, rows * STATE, 128)
    parts = [flat[k, pl.ds(start // 128 + t, rows, stride=STATE), :] for t in range(size // 128)]
    return jnp.concatenate(parts, axis=1)


def prepare(part, values, stats_ref, closed, weights, scratch):
    perm_ref, spread_ref, dt_ref, bias_ref = weights
    u_ref, d_ref, x_ref, b_ref, c_ref = scratch
    wide, tail = values
    stats = [stats_ref[r].astype(F32) for r in range(ROWS)]
    for k in range(2):
        low = jnp.concatenate([s[:, RANK * k : RANK * k + RANK] for s in stats], axis=1).astype(BF16)
        for chunk, (start, size) in enumerate(chunks_of(part)):
            cols = slice(start, start + size)
            if k == 0:
                u_ref[:, cols] = pack_rows(wide, tail, perm_ref, chunk, size)
            delta = dot(low, dt_ref[k, :, cols]) + bias_ref[k, :, cols]
            delta = jnp.maximum(delta, 0.0) + jnp.log1p(jnp.exp(-jnp.abs(delta)))
            store_tiles(x_ref, k, start, delta * u_ref[:, cols])
            if closed is not None:
                delta = jnp.where(closed[k] > 0.0, CLOSED, delta)
            store_tiles(d_ref, k, start, delta)
        for which, out_ref in ((0, b_ref), (1, c_ref)):
            at = 2 * RANK + STATE * (2 * k + which)
            picked = jnp.concatenate([s[:, at : at + STATE] for s in stats], axis=1).astype(BF16)
            for q in range(4):
                block = dot(picked, spread_ref[:, 512 * q : 512 * q + 512])
                store_tiles(out_ref, k, 512 * q, block)


def scan(k, steps, unroll, row_of, scratch, rate_ref, y_ref):
    u_ref, d_ref, x_ref, b_ref, c_ref = scratch
    tiles = u_ref.shape[1] // 128

    def step(i, state):
        row = row_of(i)
        b_now = b_ref[k, row]
        c_now = c_ref[k, row]
        after = []
        for t in range(tiles):
            cols = slice(128 * t, 128 * t + 128)
            d_now = jnp.broadcast_to(d_ref[k, row, t : t + 1, :], (STATE, 128))
            x_now = jnp.broadcast_to(x_ref[k, row, t : t + 1, :], (STATE, 128))
            h = jnp.exp2(d_now * rate_ref[k, :, cols]) * state[t] + x_now * b_now
            y_ref[k, row, t : t + 1, :] = jnp.sum(h * c_now, axis=0, keepdims=True)
            after.append(h)
        return tuple(after)

    start = tuple(jnp.zeros((STATE, 128), F32) for _ in range(tiles))
    lax.fori_loop(0, steps, step, start, unroll=unroll)


def first_kernel(x_ref, w_ref, gain_ref, proj_ref, pick_ref, inner_ref, stats_ref, tiles_ref):
    x = x_ref[0].astype(F32)
    scale = lax.rsqrt(jnp.mean(x * x, axis=1, keepdims=True) + EPSILON)
    normed = (x * scale * gain_ref[...]).astype(BF16)
    both = dot(normed, w_ref[...])

    def silu(v):
        return (v * jax.nn.sigmoid(v)).astype(BF16)

    part = inner_ref.shape[2]
    cut = part // 128 * 128
    end = part + cut
    main, last = silu(both[:, :cut]), silu(both[:, 2 * cut : end])
    inner_ref[0, :, :cut] = main
    inner_ref[0, :, cut:] = last
    stats_ref[0] = (dot(main, proj_ref[:cut, :]) + dot(last, proj_ref[cut:, :])).astype(BF16)
    pick = pick_ref[...]
    tiles_ref[0, :, :cut] = dot(pick, main).astype(BF16)
    tiles_ref[0, :, cut : 2 * cut] = dot(pick, both[:, cut : 2 * cut].astype(BF16)).astype(BF16)
    tiles_ref[0, :, 2 * cut : end] = dot(pick, last).astype(BF16)
    tiles_ref[0, :, end:] = dot(pick, both[:, end:].astype(BF16)).astype(BF16)


def spatial_kernel(
    inner_ref, stats_ref, pick_ref, perm_ref, inverse_ref, spread_ref, dt_ref, bias_ref, rate_ref,
    skip_ref, out_ref, u_ref, d_ref, x_ref, b_ref, c_ref, y_ref
):
    scratch = (u_ref, d_ref, x_ref, b_ref, c_ref)
    length, part = u_ref.shape[0], inner_ref.shape[2]
    cut = part // 128 * 128
    tail = part - cut
    values = (
        lambda r, c: inner_ref[r, :, 128 * c : 128 * c + 128],
        lambda r: inner_ref[r, :, cut:],
    )
    prepare(part, values, stats_ref, None, (perm_ref, spread_ref, dt_ref, bias_ref), scratch)
    scan(0, length, 4, lambda i: i, scratch, rate_ref, y_ref)
    scan(1, length, 4, lambda i: length - 1 - i, scratch, rate_ref, y_ref)
    pick = pick_ref[...]
    for start, size in chunks_of(part):
        cols = slice(start, start + size)
        total = load_tiles(y_ref, 0, start, size) + load_tiles(y_ref, 1, start, size)
        total = total + skip_ref[:, cols] * u_ref[:, cols]
        total = dot(pick, total.astype(BF16)).astype(BF16)
        if size == 512:
            back = dot(total, inverse_ref[...]).astype(BF16)
            for r in range(ROWS):
                at = start // 4
                out_ref[r, :, at : at + 128] = back[:, 128 * r : 128 * r + 128]
        else:
            for r in range(ROWS):
                back = dot(total, inverse_ref[0:128, 128 * r : 128 * r + tail])
                out_ref[r, :, cut:] = back.astype(BF16)


def temporal_kernel(
    frames, groups, both_ref, spatial_ref, stats_ref, closed_ref, perm_ref, inverse_ref, spread_ref,
    dt_ref, bias_ref, rate_ref, skip_ref, w_ref, out_ref, u_ref, d_ref, x_ref, b_ref, c_ref, y_ref
):
    scratch = (u_ref, d_ref, x_ref, b_ref, c_ref)
    owners, part = frames // OWN_BLK, spatial_ref.shape[2]
    cut = part // 128 * 128
    tail = part - cut
    values = (
        lambda r, c: both_ref[r, :, 128 * c : 128 * c + 128],
        lambda r: both_ref[r, :, 2 * cut : 2 * cut + tail],
    )
    closed = (closed_ref[:, 0:1], closed_ref[:, 1:2])
    prepare(part, values, stats_ref, closed, (perm_ref, spread_ref, dt_ref, bias_ref), scratch)

    def row_at(i, backward):
        group, frame = i // frames, i % frames
        if backward:
            frame = frames - 1 - frame
        return ((frame % owners) * OWN_BLK + frame // owners) * groups + group

    steps = frames * groups
    scan(0, steps, 4, lambda i: row_at(i, False), scratch, rate_ref, y_ref)
    scan(1, steps, 4, lambda i: row_at(i, True), scratch, rate_ref, y_ref)
    gate = (
        lambda r, c: both_ref[r, :, cut + 128 * c : cut + 128 * c + 128],
        lambda r: both_ref[r, :, 2 * cut + tail :],
    )
    spatial = (
        lambda r, c: spatial_ref[r, :, 128 * c : 128 * c + 128],
        lambda r: spatial_ref[r, :, cut:],
    )
    backs = []
    for chunk, (start, size) in enumerate(chunks_of(part)):
        cols = slice(start, start + size)
        total = load_tiles(y_ref, 0, start, size) + load_tiles(y_ref, 1, start, size)
        total = total + skip_ref[:, cols] * u_ref[:, cols]
        total = total + pack_rows(*spatial, perm_ref, chunk, size)
        g = pack_rows(*gate, perm_ref, chunk, size)
        total = (total * (g * jax.nn.sigmoid(g))).astype(BF16)
        if size == 512:
            backs.append(dot(total, inverse_ref[...]).astype(BF16))
        else:
            backs.append(total)
    for r in range(ROWS):
        lanes = slice(128 * r, 128 * r + 128)
        last = dot(backs[-1], inverse_ref[0:128, 128 * r : 128 * r + tail]).astype(BF16)
        term = dot(last, w_ref[cut:, :])
        for c in range(cut // 128):
            term = term + dot(backs[c][:, lanes], w_ref[128 * c : 128 * c + 128, :])
        out_ref[r] = term.astype(BF16)


def scan_scratch(rows, part):
    return [pltpu.VMEM((rows, lanes_of(part)), F32)] + [pltpu.VMEM((2, rows, STATE, 128), F32)] * 5


def call(kernel, out_shape, scratch, flops, *operands):
    return pl.pallas_call(
        kernel,
        out_shape=out_shape,
        in_specs=[pl.BlockSpec(memory_space=pltpu.VMEM)] * len(operands),
        out_specs=pl.BlockSpec(memory_space=pltpu.VMEM),
        scratch_shapes=scratch,
        compiler_params=pltpu.CompilerParams(vmem_limit_bytes=56 * 1024 * 1024),
        cost_estimate=pl.CostEstimate(flops=flops, bytes_accessed=8_000_000, transcendentals=7_000_000),
    )(*operands)


def body(
    frames_in, arrive_len, clip_len, tile_pick, norm_gain, in_weight, proj_weight, dt_weight, dt_bias,
    decay_rate, skip_gain, out_weight
):
    owners = lax.axis_size("tm")
    my_owner = lax.axis_index("tm")
    space_index = lax.axis_index("space")
    patches = PATCHES
    width = in_weight.shape[1]
    part = out_weight.shape[0]
    cut = part // 128 * 128
    frames_total = owners * OWN_BLK
    per_owner = tile_pick.shape[1] // owners
    groups = -(-per_owner // ROWS)
    slots = ROWS * groups

    weight = lax.dynamic_slice_in_dim(in_weight, space_index * part, part, 2)
    weight = jnp.concatenate(
        [weight[0, :, :cut], weight[1, :, :cut], weight[0, :, cut:], weight[1, :, cut:]], axis=1
    )
    widen = jnp.asarray(widening(part))
    exact = functools.partial(
        jnp.einsum, precision=lax.Precision.HIGHEST, preferred_element_type=F32
    )
    rate = exact("kcs,cn->ksn", decay_rate, widen) * -LOG2E
    bias = exact("kc,cn->kn", dt_bias, widen)[:, None, :]
    skip = exact("kc,cn->kn", skip_gain, widen)
    dt_wide = jnp.einsum(
        "kic,cn->kin", dt_weight, widen.astype(BF16), preferred_element_type=F32
    ).astype(BF16)
    lane_row = (jnp.arange(lanes_of(part), dtype=jnp.int32) % 128) // 32
    same = (lane_row[None, :] == jnp.arange(ROWS, dtype=jnp.int32)[:, None])[None, :, None, :]
    dt_wide = jnp.where(same, dt_wide[:, None], jnp.zeros((), BF16)).reshape(4, ROWS * RANK, lanes_of(part))
    pieces = []
    for half in (0, 2):
        pieces += [proj_weight[half, :, :RANK], proj_weight[half + 1, :, :RANK]]
        pieces += [proj_weight[half, :, RANK:], proj_weight[half + 1, :, RANK:]]
    proj = jnp.concatenate(pieces, axis=1)
    pick = tile_pick.astype(BF16).T.reshape(owners, per_owner, patches)
    pick = jnp.pad(pick, ((0, 0), (0, slots - per_owner), (0, 0))).reshape(owners * slots, patches)
    perm, inverse = jnp.asarray(PERM, BF16), jnp.asarray(PERM.T, BF16)
    spread = jnp.asarray(SPREAD, BF16)

    capacity = (IN_BLK + owners - 1) // owners
    offsets = jnp.cumsum(arrive_len) - arrive_len
    lane_index = jnp.arange(capacity, dtype=jnp.int32)[None, :]
    target_ids = jnp.arange(owners, dtype=jnp.int32)[:, None]
    slot_index = (target_ids - offsets[my_owner]) % owners + lane_index * owners
    packed = jnp.take(frames_in, jnp.minimum(slot_index, IN_BLK - 1).reshape(-1), axis=0)
    arrived = lax.all_to_all(packed, "tm", split_axis=0, concat_axis=0, tiled=True)
    wanted = jnp.arange(OWN_BLK, dtype=jnp.int32) * owners + my_owner
    sender = jnp.sum((offsets[None, :] <= wanted[:, None]).astype(jnp.int32), axis=1) - 1
    lane_of = (wanted - offsets[sender]) // owners
    owned = jnp.take(arrived, sender * capacity + lane_of, axis=0)
    full = lax.all_gather(owned, "space", axis=1, tiled=True).reshape(OWN_BLK, patches, width)

    inner, stats, tiles = pl.pallas_call(
        first_kernel,
        grid=(OWN_BLK,),
        out_shape=(
            jax.ShapeDtypeStruct((OWN_BLK, patches, part), BF16),
            jax.ShapeDtypeStruct((OWN_BLK, patches, 2 * HALF), BF16),
            jax.ShapeDtypeStruct((OWN_BLK, owners * slots, 2 * part), BF16),
        ),
        in_specs=[
            pl.BlockSpec((1, patches, width), lambda i: (i, 0, 0)),
            pl.BlockSpec((width, 2 * part), lambda i: (0, 0)),
            pl.BlockSpec((1, width), lambda i: (0, 0)),
            pl.BlockSpec((part, 2 * HALF), lambda i: (0, 0)),
            pl.BlockSpec((owners * slots, patches), lambda i: (0, 0)),
        ],
        out_specs=(
            pl.BlockSpec((1, patches, part), lambda i: (i, 0, 0)),
            pl.BlockSpec((1, patches, 2 * HALF), lambda i: (i, 0, 0)),
            pl.BlockSpec((1, owners * slots, 2 * part), lambda i: (i, 0, 0)),
        ),
        compiler_params=pltpu.CompilerParams(vmem_limit_bytes=32 * 1024 * 1024),
        cost_estimate=pl.CostEstimate(flops=900_000_000, bytes_accessed=4_000_000, transcendentals=250_000),
    )(full, weight, norm_gain[None, :], proj, pick)
    stats = lax.psum(stats, "space")

    def to_owner(array):
        moved = lax.all_to_all(array, "tm", split_axis=1, concat_axis=0, tiled=True)
        moved = moved.reshape(frames_total, ROWS, groups, array.shape[-1])
        return jnp.swapaxes(moved, 0, 1).reshape(ROWS, frames_total * groups, array.shape[-1])

    time_both = to_owner(tiles)
    late = jnp.einsum("sp,lpc->lsc", pick, stats[:, :, HALF:], preferred_element_type=F32)
    time_stats = to_owner(late.astype(BF16))
    spatial = call(
        spatial_kernel,
        jax.ShapeDtypeStruct((OWN_BLK, owners * slots, part), BF16),
        scan_scratch(patches, part),
        600_000_000,
        inner, stats[:, :, :HALF], pick, perm, inverse, spread, dt_wide[:2], bias[:2], rate[:2],
        (skip[0] + skip[1])[None, :],
    )
    time_spatial = to_owner(spatial)

    clip_start = jnp.cumsum(clip_len) - clip_len
    row_frame = jnp.arange(frames_total, dtype=jnp.int32)
    row_frame = (row_frame % OWN_BLK) * owners + row_frame // OWN_BLK
    opens = jnp.any(row_frame[:, None] == clip_start[None, :], axis=1) | (row_frame == 0)
    closes = jnp.any(row_frame[:, None] == (clip_start + clip_len - 1)[None, :], axis=1)
    closes = closes | (row_frame == frames_total - 1)
    closed = jnp.stack([opens, closes], axis=1).astype(F32)
    closed = jnp.repeat(closed, groups, axis=0)
    rows = frames_total * groups
    term = call(
        functools.partial(temporal_kernel, frames_total, groups),
        jax.ShapeDtypeStruct((ROWS, rows, width), BF16),
        scan_scratch(rows, part),
        600_000_000,
        time_both, time_spatial, time_stats, closed, perm, inverse, spread, dt_wide[2:], bias[2:],
        rate[2:], (skip[2] + skip[3])[None, :], out_weight,
    )
    term = term.reshape(ROWS, owners, OWN_BLK, groups, width)
    term = jnp.transpose(term, (0, 3, 2, 1, 4)).reshape(slots, frames_total * width)[:per_owner]
    return lax.psum_scatter(term, "space", scatter_dimension=1, tiled=True)


def solution(mesh):
    placed = (
        P(("groups", "tm"), "space"),
        P("groups"),
        P("groups"),
        P("groups", None),
        P(),
        P(),
        P(None, "space", None),
        P(None, None, "space"),
        P(None, "space"),
        P(None, "space", None),
        P(None, "space"),
        P("space", None),
    )
    return jax.shard_map(
        body, mesh=mesh, in_specs=placed, out_specs=P("tm", ("groups", "space")), check_vma=False
    )
```

profile of v0, /device:TPU:0, one launch (start us, length us, event | category | flops | bytes accessed | tf_op | source)
XLA Modules:
  0.0 228.8 jit_solution(13580729604515190011)
XLA Ops:
  6.5 0.9 reduce-window.16
  7.4 0.7 bitcast_subtract_fusion.2
  8.1 0.6 dynamic_slice.6
  8.7 0.7 and_select_fusion.5
  9.6 0.8 gather_fusion.1
  10.6 1.2 broadcast_select_fusion.1
  11.9 6.3 %all-to-all-start = ((bf16[4,2,28224]{2,1,0:T(2,128)(2,1)}), bf16[4,2,28224]{2,1,0:T(2,128)(2,1)S(1)}, u32[]{:S(2)}, u32[]{:S(2)}) async-start(bf16[4,2,28224]{2,1,0:T(2,128)(2,1)} %broadcast_select_fusion.1), calls=%async_computation | async-start | bytes 905216 | tf_op jit(solution)/shard_map/all_to_all | solution.py:306
  18.7 0.7 reshape.407.pick_ref
  19.4 0.7 reshape.448
  20.3 0.6 gather_fusion
  21.0 1.5 dynamic-slice_bitcast_fusion.1
  22.4 1.1 dynamic-slice_bitcast_fusion.3
  24.5 0.8 copy.163
  25.3 0.8 copy.164
  26.1 1.5 fusion
  27.7 0.6 broadcast_select_fusion
  28.3 1.8 fusion.19
  30.1 0.9 copy.137.dt_ref
  31.0 0.6 copy-done.4
  31.6 0.8 convolution_bitcast_fusion.1
  32.4 0.6 copy.138.bias_ref
  33.0 1.1 fusion.24
  34.3 1.2 concatenate.7.proj_ref
  35.6 0.7 fusion.20
  36.3 0.3 all_to_all.40
  36.6 0.8 gather_fusion.2
  37.6 9.4 %all-gather = bf16[4,28224,4]{1,2,0:T(4,128)(2,1)S(1)} all-gather(bf16[1,28224,4]{1,2,0:T(4,128)(2,1)S(1)} %select_bitcast_fusion), channel_id=1, replica_groups=mesh['groups'=2,'tm'=4,'space'=4] {'space'}, dimensions={0}, use_global_device_ids=true | all-gather | bytes 1128960 | tf_op jit(solution)/shard_map/all_gather | solution.py:311
  47.0 0.3 copy.122
  47.3 0.9 reshape.444
  48.2 0.8 reshape.405.x_ref
  49.1 0.9 copy-done.2
  49.9 3.5 %shard_map.154 = (bf16[4,196,288]{2,1,0:T(8,128)(2,1)S(1)}, bf16[4,196,272]{2,1,0:T(8,128)(2,1)S(1)}, bf16[4,208,576]{2,1,0:T(8,128)(2,1)S(1)}) custom-call(bf16[4,196,576]{2,1,0:T(8,128)(2,1)S(1)} %reshape.405.x_ref, bf16[576,576]{1,0:T(8,128)(2,1)S(1)} %pad_maximum_fusion.w_ref, f32[1,576]{1,0:T(1,128)S(1)} %broadcast_in_dim.66.gain_ref, ...), custom_call_target="tpu_custom_call" | custom-call | flops 900000000 | bytes 4000000 | tf_op jit(solution)/shard_map/pallas_call | solution.py:313
  53.5 0.8 copy-done.1
  54.3 0.8 copy-done.3
  55.2 2.2 convolution_bitcast_fusion
  57.3 32.2 %all-reduce.3.cloned.1.call-done = bf16[4,196,272]{2,1,0:T(8,128)(2,1)} async-done(((bf16[4,196,272]{2,1,0:T(8,128)(2,1)}), bf16[4,196,272]{2,1,0:T(8,128)(2,1)}) %all-reduce.3.cloned.1.call-update) | async-done | bytes 426512 | tf_op jit(solution)/shard_map/psum | solution.py:336
  89.5 1.6 fusion.1
  91.1 1.0 copy.143
  92.1 4.6 %all-to-all-start.3 = ((bf16[4,208,136]{2,0,1:T(4,128)(2,1)}), bf16[4,208,136]{2,0,1:T(4,128)(2,1)S(1)}, u32[]{:S(2)}, u32[]{:S(2)}) async-start(bf16[4,208,136]{2,0,1:T(4,128)(2,1)} %copy.143), calls=%async_computation.3 | async-start | bytes 851968 | tf_op jit(solution)/shard_map/all_to_all | solution.py:339
  96.7 0.6 slice_add_fusion
  97.3 0.8 slice.122.stats_ref
  98.1 18.4 %shard_map.155 = bf16[4,208,288]{2,1,0:T(8,128)(2,1)} custom-call(bf16[4,196,288]{2,1,0:T(8,128)(2,1)} %copy-done.3, bf16[4,196,136]{2,1,0:T(8,128)(2,1)} %slice.122.stats_ref, bf16[208,196]{1,0:T(8,128)(2,1)} %reshape.407.pick_ref, bf16[512,512]{1,0:T(8,128)(2,1)} %constant.150.clone.perm_ref.inverse_ref, ...), custom_call_target="tpu_custom_call" | custom-call | flops 600000000 | bytes 8000000 | tf_op jit(solution)/shard_map/pallas_call | solution.py:246
  116.5 2.2 copy.139
  118.7 5.1 %all-to-all-start.2 = ((bf16[4,208,288]{2,0,1:T(4,128)(2,1)}), bf16[4,208,288]{2,0,1:T(4,128)(2,1)S(1)}, u32[]{:S(2)}, u32[]{:S(2)}) async-start(bf16[4,208,288]{2,0,1:T(4,128)(2,1)} %copy.139), calls=%async_computation.2 | async-start | bytes 1277952 | tf_op jit(solution)/shard_map/all_to_all | solution.py:339
  123.8 1.4 copy.132
  125.2 14.2 %all-to-all-done.2 = bf16[4,208,288]{2,0,1:T(4,128)(2,1)S(1)} async-done(((bf16[4,208,288]{2,0,1:T(4,128)(2,1)}), bf16[4,208,288]{2,0,1:T(4,128)(2,1)S(1)}, u32[]{:S(2)}, u32[]{:S(2)}) %all-to-all-start.2) | async-done | bytes 479264 | tf_op jit(solution)/shard_map/all_to_all | solution.py:339
  139.4 3.5 %all-to-all-start.1 = ((bf16[4,208,576]{2,0,1:T(4,128)(2,1)}), bf16[4,208,576]{2,0,1:T(4,128)(2,1)S(1)}, u32[]{:S(2)}, u32[]{:S(2)}) async-start(bf16[4,208,576]{2,0,1:T(4,128)(2,1)} %copy.132), calls=%async_computation.1 | async-start | bytes 2129920 | tf_op jit(solution)/shard_map/all_to_all | solution.py:339
  142.9 0.3 reduce-scatter.2.cloned.1.call-start
  143.7 0.8 copy.150.closed_ref
  144.5 0.9 copy.151.dt_ref
  145.4 0.6 slice.111.bias_ref
  146.6 0.8 copy.149.stats_ref
  147.7 0.3 reshape.410
  148.3 0.9 copy.148.spatial_ref
  149.2 19.3 %all-to-all-done.1 = bf16[4,208,576]{2,0,1:T(4,128)(2,1)S(1)} async-done(((bf16[4,208,576]{2,0,1:T(4,128)(2,1)}), bf16[4,208,576]{2,0,1:T(4,128)(2,1)S(1)}, u32[]{:S(2)}, u32[]{:S(2)}) %all-to-all-start.1) | async-done | bytes 958496 | tf_op jit(solution)/shard_map/all_to_all | solution.py:339
  168.4 0.4 copy.133
  168.8 0.6 reshape.408
  169.4 0.4 copy.134
  169.8 1.1 copy.147.both_ref
  170.9 23.2 %shard_map.156 = bf16[4,208,576]{2,1,0:T(8,128)(2,1)} custom-call(bf16[4,208,576]{2,1,0:T(8,128)(2,1)} %copy.147.both_ref, bf16[4,208,288]{2,1,0:T(8,128)(2,1)} %copy.148.spatial_ref, bf16[4,208,136]{2,1,0:T(8,128)(2,1)} %copy.149.stats_ref, f32[208,2]{1,0:T(8,128)} %copy.150.closed_ref, bf16[512,512]{1,0:T(8,128)(2,1)} %constant.150.clone.perm_ref.inverse_ref, ...), custom_call_target="tpu_custom_call" | custom-call | flops 600000000 | bytes 8000000 | tf_op jit(solution)/shard_map/pallas_call | solution.py:246
  194.1 1.6 copy.152
  195.8 0.4 copy.153
  196.2 2.2 reshape.418
  198.4 23.5 %reduce-scatter.2.cloned.1.call-done = bf16[49,2304]{1,0:T(8,128)(2,1)} async-done(((bf16[49,9216]{1,0:T(8,128)(2,1)}), bf16[49,2304]{1,0:T(8,128)(2,1)}) %reduce-scatter.2.cloned.1.call-update) | async-done | bytes 225808 | tf_op jit(solution)/shard_map/reduce_scatter | solution.py:375
  (79 shorter events, 4.2 us)
Async XLA Ops:
  6.5 3.0 %copy-start = (bf16[8,28224]{1,0:T(8,128)(2,1)S(1)}, bf16[8,28224]{1,0:T(8,128)(2,1)}, u32[]{:S(2)}) copy-start(bf16[8,28224]{1,0:T(8,128)(2,1)} %param.16) | copy-start | bytes 1354756
  10.4 7.7 %copy-start.7 = (bf16[4,288,68]{1,0,2:T(4,128)(2,1)S(1)}, bf16[4,288,68]{1,0,2:T(4,128)(2,1)}, u32[]{:S(2)}) copy-start(bf16[4,288,68]{1,0,2:T(4,128)(2,1)} %param.22) | copy-start | bytes 470020
  10.6 7.9 %copy-start.9 = (s32[196,196]{1,0:T(8,128)S(1)}, s32[196,196]{1,0:T(8,128)}, u32[]{:S(2)}) copy-start(s32[196,196]{1,0:T(8,128)} %param.19) | copy-start | bytes 460996
  11.9 24.5 %all-to-all-start = ((bf16[4,2,28224]{2,1,0:T(2,128)(2,1)}), bf16[4,2,28224]{2,1,0:T(2,128)(2,1)S(1)}, u32[]{:S(2)}, u32[]{:S(2)}) async-start(bf16[4,2,28224]{2,1,0:T(2,128)(2,1)} %broadcast_select_fusion.1), calls=%async_computation | async-start | bytes 905216 | tf_op jit(solution)/shard_map/all_to_all | solution.py:306
  18.2 71.3 %all-reduce.3.cloned.1.call-start = ((), (), s32[]{:S(2)}) async-start(), calls=%async_computation.5 | async-start | bytes 1228800 | tf_op jit(solution)/shard_map/psum | solution.py:336
  19.4 4.2 %copy-start.13 = (f32[576]{0:T(1024)S(1)}, f32[576]{0:T(1024)}, u32[]{:S(2)}) copy-start(f32[576]{0:T(1024)} %param.20) | copy-start | bytes 6916
  21.0 5.1 %copy-start.15 = (bf16[4,36,288]{2,0,1:T(4,128)(2,1)S(1)}, bf16[4,36,288]{2,0,1:T(4,128)(2,1)}, u32[]{:S(2)}) copy-start(bf16[4,36,288]{2,0,1:T(4,128)(2,1)} %param.23) | copy-start | bytes 248836
  28.2 2.8 %copy-start.11 = (f32[4,288]{1,0:T(4,128)S(1)}, f32[4,288]{1,0:T(4,128)}, u32[]{:S(2)}) copy-start(f32[4,288]{1,0:T(4,128)} %param.24) | copy-start | bytes 13828
  30.1 1.6 copy-start.4
  30.1 3.0 %copy-start.10 = (f32[4,288,16]{1,2,0:T(8,128)S(1)}, f32[4,288,16]{1,2,0:T(8,128)}, u32[]{:S(2)}) copy-start(f32[4,288,16]{1,2,0:T(8,128)} %param.25) | copy-start | bytes 221188
  49.0 0.9 copy-start.2
  49.9 5.2 %copy-start.12 = (f32[4,288]{1,0:T(4,128)S(1)}, f32[4,288]{1,0:T(4,128)}, u32[]{:S(2)}) copy-start(f32[4,288]{1,0:T(4,128)} %param.26) | copy-start | bytes 13828
  53.5 0.8 copy-start.1
  54.3 0.8 copy-start.3
  55.1 34.4 %copy-start.8 = (bf16[208,196,1]{1,0,2:T(8,128)(2,1)S(1)}, bf16[208,196,1]{1,0,2:T(8,128)(2,1)}, u32[]{:S(2)}) copy-start(bf16[208,196,1]{1,0,2:T(8,128)(2,1)} %reshape.448) | copy-start | bytes 244612
  89.5 7.8 %copy-start.6 = (bf16[4,196,272]{2,1,0:T(8,128)(2,1)S(1)}, bf16[4,196,272]{2,1,0:T(8,128)(2,1)}, u32[]{:S(2)}) copy-start(bf16[4,196,272]{2,1,0:T(8,128)(2,1)} %all-reduce.3.cloned.1.call-done) | copy-start | bytes 1279492
  92.1 26.6 %all-to-all-start.3 = ((bf16[4,208,136]{2,0,1:T(4,128)(2,1)}), bf16[4,208,136]{2,0,1:T(4,128)(2,1)S(1)}, u32[]{:S(2)}, u32[]{:S(2)}) async-start(bf16[4,208,136]{2,0,1:T(4,128)(2,1)} %copy.143), calls=%async_computation.3 | async-start | bytes 851968 | tf_op jit(solution)/shard_map/all_to_all | solution.py:339
  118.7 20.7 %all-to-all-start.2 = ((bf16[4,208,288]{2,0,1:T(4,128)(2,1)}), bf16[4,208,288]{2,0,1:T(4,128)(2,1)S(1)}, u32[]{:S(2)}, u32[]{:S(2)}) async-start(bf16[4,208,288]{2,0,1:T(4,128)(2,1)} %copy.139), calls=%async_computation.2 | async-start | bytes 1277952 | tf_op jit(solution)/shard_map/all_to_all | solution.py:339
  125.2 18.0 %copy-start.14 = (s32[4]{0:T(128)S(1)}, s32[4]{0:T(128)}, u32[]{:S(2)}) copy-start(s32[4]{0:T(128)} %param.18) | copy-start | bytes 52
  125.2 19.3 %copy-start.5 = (bf16[2,4,36,1152]{3,0,2,1:T(2,128)(2,1)S(1)}, bf16[2,4,36,1152]{3,0,2,1:T(2,128)(2,1)}, u32[]{:S(2)}) copy-start(bf16[2,4,36,1152]{3,0,2,1:T(2,128)(2,1)} %get-tuple-element.17) | copy-start | bytes 1990660
  139.4 29.0 %all-to-all-start.1 = ((bf16[4,208,576]{2,0,1:T(4,128)(2,1)}), bf16[4,208,576]{2,0,1:T(4,128)(2,1)S(1)}, u32[]{:S(2)}, u32[]{:S(2)}) async-start(bf16[4,208,576]{2,0,1:T(4,128)(2,1)} %copy.132), calls=%async_computation.1 | async-start | bytes 2129920 | tf_op jit(solution)/shard_map/all_to_all | solution.py:339
  142.9 79.0 %reduce-scatter.2.cloned.1.call-start = ((), (), s32[]{:S(2)}) async-start(), calls=%async_computation.6 | async-start | bytes 1290240 | tf_op jit(solution)/shard_map/reduce_scatter | solution.py:375
Sparse Core Ops, SparseCore 0:
  55.3 34.1 all-reduce.2
  198.5 23.3 reduce-scatter.1
where the time goes:
time: 230 us; the launch traced here: 229 us
  waiting for transfers between devices  89.2 us (39%)
  Pallas kernels  45.1 us (20%)
  local copies, waits for them, and re-layouts  38.6 us (17%)
  starting transfers between devices  19.8 us (9%)
  between operations  13.8 us (6%)
  blocking collectives  9.42 us (4%)
  matrix products  7.1 us (3%)
  other arithmetic  5.65 us (2%)
    pallas_call x2, Pallas kernels, call(): pl.pallas_call(kernel, out_shape=out_shape, in_specs=[pl.BlockSpec(memory...  41.6 us
    all_to_all x3, waiting for transfers between devices, to_owner(): moved = lax.all_to_all(array, 'tm', split_axis=1, concat_axis=0, tiled=True)  33.5 us
    psum x1, waiting for transfers between devices, body(): stats = lax.psum(stats, 'space')  32.2 us
    reduce_scatter x1, waiting for transfers between devices, body(): return lax.psum_scatter(term, 'space', scatter_dimension=1, tiled=True)  23.5 us
    all_to_all x3, starting transfers between devices, to_owner(): moved = lax.all_to_all(array, 'tm', split_axis=1, concat_axis=0, tiled=True)  13.2 us
    all_gather x1, blocking collectives, body(): lax.all_gather(owned, 'space', axis=1, tiled=True)  9.42 us
    unnamed x41, local copies, waits for them, and re-layouts  6.51 us
    all_to_all x1, starting transfers between devices, body(): lax.all_to_all(packed, 'tm', split_axis=0, concat_axis=0, tiled=True)  6.32 us
  transfers between devices with their start and end apart: 6, of which 4 were waited for; matrix products, arithmetic and copies ran while one was open for 13% of the time, Pallas kernels for 8%

commit v1 on v0

--- a/solution.py
+++ b/solution.py
@@ -83,11 +83,11 @@
     return jnp.concatenate(parts, axis=1)
 
 
-def prepare(part, values, stats_ref, closed, weights, scratch):
+def prepare(part, values, stats_ref, base, closed, weights, scratch):
     perm_ref, spread_ref, dt_ref, bias_ref = weights
     u_ref, d_ref, x_ref, b_ref, c_ref = scratch
     wide, tail = values
-    stats = [stats_ref[r].astype(F32) for r in range(ROWS)]
+    stats = [stats_ref[r, :, base : base + HALF].astype(F32) for r in range(ROWS)]
     for k in range(2):
         low = jnp.concatenate([s[:, RANK * k : RANK * k + RANK] for s in stats], axis=1).astype(BF16)
         for chunk, (start, size) in enumerate(chunks_of(part)):
@@ -130,31 +130,31 @@
     lax.fori_loop(0, steps, step, start, unroll=unroll)
 
 
-def first_kernel(x_ref, w_ref, gain_ref, proj_ref, pick_ref, inner_ref, stats_ref, tiles_ref):
+def silu(v):
+    return v * jax.nn.sigmoid(v)
+
+
+def first_kernel(
+    x_ref, w_ref, all_ref, gain_ref, proj_ref, pick_ref, inner_ref, stats_ref, tiles_ref, gate_ref
+):
     x = x_ref[0].astype(F32)
     scale = lax.rsqrt(jnp.mean(x * x, axis=1, keepdims=True) + EPSILON)
     normed = (x * scale * gain_ref[...]).astype(BF16)
-    both = dot(normed, w_ref[...])
-
-    def silu(v):
-        return (v * jax.nn.sigmoid(v)).astype(BF16)
-
     part = inner_ref.shape[2]
-    cut = part // 128 * 128
-    end = part + cut
-    main, last = silu(both[:, :cut]), silu(both[:, 2 * cut : end])
-    inner_ref[0, :, :cut] = main
-    inner_ref[0, :, cut:] = last
-    stats_ref[0] = (dot(main, proj_ref[:cut, :]) + dot(last, proj_ref[cut:, :])).astype(BF16)
+    inner = silu(dot(normed, w_ref[0])).astype(BF16)
+    gate = dot(normed, w_ref[1]).astype(BF16)
+    inner_ref[0] = inner
+    whole = silu(dot(normed, all_ref[0])).astype(BF16)
+    stats = dot(whole, proj_ref[...]).astype(BF16)
+    stats_ref[0] = stats[:, :HALF]
     pick = pick_ref[...]
-    tiles_ref[0, :, :cut] = dot(pick, main).astype(BF16)
-    tiles_ref[0, :, cut : 2 * cut] = dot(pick, both[:, cut : 2 * cut].astype(BF16)).astype(BF16)
-    tiles_ref[0, :, 2 * cut : end] = dot(pick, last).astype(BF16)
-    tiles_ref[0, :, end:] = dot(pick, both[:, end:].astype(BF16)).astype(BF16)
+    tiles_ref[0, :, :part] = dot(pick, inner).astype(BF16)
+    tiles_ref[0, :, part:] = dot(pick, stats[:, HALF:]).astype(BF16)
+    gate_ref[0] = dot(pick, gate).astype(BF16)
 
 
 def spatial_kernel(
-    inner_ref, stats_ref, pick_ref, perm_ref, inverse_ref, spread_ref, dt_ref, bias_ref, rate_ref,
+    inner_ref, stats_ref, gate_ref, pick_ref, perm_ref, inverse_ref, spread_ref, dt_ref, bias_ref, rate_ref,
     skip_ref, out_ref, u_ref, d_ref, x_ref, b_ref, c_ref, y_ref
 ):
     scratch = (u_ref, d_ref, x_ref, b_ref, c_ref)
@@ -165,7 +165,7 @@
         lambda r, c: inner_ref[r, :, 128 * c : 128 * c + 128],
         lambda r: inner_ref[r, :, cut:],
     )
-    prepare(part, values, stats_ref, None, (perm_ref, spread_ref, dt_ref, bias_ref), scratch)
+    prepare(part, values, stats_ref, 0, None, (perm_ref, spread_ref, dt_ref, bias_ref), scratch)
     scan(0, length, 4, lambda i: i, scratch, rate_ref, y_ref)
     scan(1, length, 4, lambda i: length - 1 - i, scratch, rate_ref, y_ref)
     pick = pick_ref[...]
@@ -182,23 +182,25 @@
         else:
             for r in range(ROWS):
                 back = dot(total, inverse_ref[0:128, 128 * r : 128 * r + tail])
-                out_ref[r, :, cut:] = back.astype(BF16)
+                out_ref[r, :, 2 * cut : 2 * cut + tail] = back.astype(BF16)
+    for r in range(ROWS):
+        out_ref[r, :, cut : 2 * cut] = gate_ref[r, :, :cut]
+        out_ref[r, :, 2 * cut + tail :] = gate_ref[r, :, cut:]
 
 
 def temporal_kernel(
-    frames, groups, both_ref, spatial_ref, stats_ref, closed_ref, perm_ref, inverse_ref, spread_ref,
-    dt_ref, bias_ref, rate_ref, skip_ref, w_ref, out_ref, u_ref, d_ref, x_ref, b_ref, c_ref, y_ref
+    frames, groups, part, moved_ref, closed_ref, perm_ref, spread_ref, dt_ref, bias_ref, rate_ref,
+    skip_ref, out_ref, u_ref, d_ref, x_ref, b_ref, c_ref, y_ref
 ):
     scratch = (u_ref, d_ref, x_ref, b_ref, c_ref)
-    owners, part = frames // OWN_BLK, spatial_ref.shape[2]
+    owners = frames // OWN_BLK
     cut = part // 128 * 128
-    tail = part - cut
     values = (
-        lambda r, c: both_ref[r, :, 128 * c : 128 * c + 128],
-        lambda r: both_ref[r, :, 2 * cut : 2 * cut + tail],
+        lambda r, c: moved_ref[r, :, 128 * c : 128 * c + 128],
+        lambda r: moved_ref[r, :, cut:part],
     )
     closed = (closed_ref[:, 0:1], closed_ref[:, 1:2])
-    prepare(part, values, stats_ref, closed, (perm_ref, spread_ref, dt_ref, bias_ref), scratch)
+    prepare(part, values, moved_ref, part, closed, (perm_ref, spread_ref, dt_ref, bias_ref), scratch)
 
     def row_at(i, backward):
         group, frame = i // frames, i % frames
@@ -209,26 +211,31 @@
     steps = frames * groups
     scan(0, steps, 4, lambda i: row_at(i, False), scratch, rate_ref, y_ref)
     scan(1, steps, 4, lambda i: row_at(i, True), scratch, rate_ref, y_ref)
+    for start, size in chunks_of(part):
+        cols = slice(start, start + size)
+        total = load_tiles(y_ref, 0, start, size) + load_tiles(y_ref, 1, start, size)
+        out_ref[:, cols] = total + skip_ref[:, cols] * u_ref[:, cols]
+
+
+def output_kernel(temporal_ref, moved_ref, perm_ref, inverse_ref, w_ref, out_ref):
+    part = w_ref.shape[0]
+    cut = part // 128 * 128
+    tail = part - cut
+    spatial = (
+        lambda r, c: moved_ref[r, :, 128 * c : 128 * c + 128],
+        lambda r: moved_ref[r, :, 2 * cut : 2 * cut + tail],
+    )
     gate = (
-        lambda r, c: both_ref[r, :, cut + 128 * c : cut + 128 * c + 128],
-        lambda r: both_ref[r, :, 2 * cut + tail :],
-    )
-    spatial = (
-        lambda r, c: spatial_ref[r, :, 128 * c : 128 * c + 128],
-        lambda r: spatial_ref[r, :, cut:],
+        lambda r, c: moved_ref[r, :, cut + 128 * c : cut + 128 * c + 128],
+        lambda r: moved_ref[r, :, 2 * cut + tail :],
     )
     backs = []
     for chunk, (start, size) in enumerate(chunks_of(part)):
-        cols = slice(start, start + size)
-        total = load_tiles(y_ref, 0, start, size) + load_tiles(y_ref, 1, start, size)
-        total = total + skip_ref[:, cols] * u_ref[:, cols]
-        total = total + pack_rows(*spatial, perm_ref, chunk, size)
-        g = pack_rows(*gate, perm_ref, chunk, size)
-        total = (total * (g * jax.nn.sigmoid(g))).astype(BF16)
+        total = temporal_ref[:, start : start + size] + pack_rows(*spatial, perm_ref, chunk, size)
+        total = (total * silu(pack_rows(*gate, perm_ref, chunk, size))).astype(BF16)
         if size == 512:
-            backs.append(dot(total, inverse_ref[...]).astype(BF16))
-        else:
-            backs.append(total)
+            total = dot(total, inverse_ref[...]).astype(BF16)
+        backs.append(total)
     for r in range(ROWS):
         lanes = slice(128 * r, 128 * r + 128)
         last = dot(backs[-1], inverse_ref[0:128, 128 * r : 128 * r + tail]).astype(BF16)
@@ -264,16 +271,12 @@
     patches = PATCHES
     width = in_weight.shape[1]
     part = out_weight.shape[0]
-    cut = part // 128 * 128
     frames_total = owners * OWN_BLK
     per_owner = tile_pick.shape[1] // owners
     groups = -(-per_owner // ROWS)
     slots = ROWS * groups
 
     weight = lax.dynamic_slice_in_dim(in_weight, space_index * part, part, 2)
-    weight = jnp.concatenate(
-        [weight[0, :, :cut], weight[1, :, :cut], weight[0, :, cut:], weight[1, :, cut:]], axis=1
-    )
     widen = jnp.asarray(widening(part))
     exact = functools.partial(
         jnp.einsum, precision=lax.Precision.HIGHEST, preferred_element_type=F32
@@ -292,6 +295,13 @@
         pieces += [proj_weight[half, :, :RANK], proj_weight[half + 1, :, :RANK]]
         pieces += [proj_weight[half, :, RANK:], proj_weight[half + 1, :, RANK:]]
     proj = jnp.concatenate(pieces, axis=1)
+    spaces = lax.axis_size("space")
+    shares = [proj] + [
+        lax.ppermute(proj, "space", [(i, (i + k) % spaces) for i in range(spaces)])
+        for k in range(1, spaces)
+    ]
+    order = (space_index - jnp.arange(spaces, dtype=jnp.int32)) % spaces
+    proj = jnp.take(jnp.stack(shares), order, axis=0).reshape(spaces * part, 2 * HALF)
     pick = tile_pick.astype(BF16).T.reshape(owners, per_owner, patches)
     pick = jnp.pad(pick, ((0, 0), (0, slots - per_owner), (0, 0))).reshape(owners * slots, patches)
     perm, inverse = jnp.asarray(PERM, BF16), jnp.asarray(PERM.T, BF16)
@@ -310,48 +320,52 @@
     owned = jnp.take(arrived, sender * capacity + lane_of, axis=0)
     full = lax.all_gather(owned, "space", axis=1, tiled=True).reshape(OWN_BLK, patches, width)
 
-    inner, stats, tiles = pl.pallas_call(
+    def per_frame(*dims):
+        return pl.BlockSpec((1,) + dims, lambda i: (i, 0, 0))
+
+    def same_each(array):
+        return pl.BlockSpec(array.shape, lambda i: (0,) * array.ndim)
+
+    rests = (weight, in_weight, norm_gain[None, :], proj, pick)
+    inner, stats, tiles, gate = pl.pallas_call(
         first_kernel,
         grid=(OWN_BLK,),
         out_shape=(
             jax.ShapeDtypeStruct((OWN_BLK, patches, part), BF16),
-            jax.ShapeDtypeStruct((OWN_BLK, patches, 2 * HALF), BF16),
-            jax.ShapeDtypeStruct((OWN_BLK, owners * slots, 2 * part), BF16),
+            jax.ShapeDtypeStruct((OWN_BLK, patches, HALF), BF16),
+            jax.ShapeDtypeStruct((OWN_BLK, owners * slots, part + HALF), BF16),
+            jax.ShapeDtypeStruct((OWN_BLK, owners * slots, part), BF16),
         ),
-        in_specs=[
-            pl.BlockSpec((1, patches, width), lambda i: (i, 0, 0)),
-            pl.BlockSpec((width, 2 * part), lambda i: (0, 0)),
-            pl.BlockSpec((1, width), lambda i: (0, 0)),
-            pl.BlockSpec((part, 2 * HALF), lambda i: (0, 0)),
-            pl.BlockSpec((owners * slots, patches), lambda i: (0, 0)),
-        ],
+        in_specs=[per_frame(patches, width), same_each(weight)]
+        + [pl.BlockSpec((1,) + in_weight.shape[1:], lambda i: (0, 0, 0))]
+        + [same_each(a) for a in rests[2:]],
         out_specs=(
-            pl.BlockSpec((1, patches, part), lambda i: (i, 0, 0)),
-            pl.BlockSpec((1, patches, 2 * HALF), lambda i: (i, 0, 0)),
-            pl.BlockSpec((1, owners * slots, 2 * part), lambda i: (i, 0, 0)),
+            per_frame(patches, part),
+            per_frame(patches, HALF),
+            per_frame(owners * slots, part + HALF),
+            per_frame(owners * slots, part),
         ),
-        compiler_params=pltpu.CompilerParams(vmem_limit_bytes=32 * 1024 * 1024),
-        cost_estimate=pl.CostEstimate(flops=900_000_000, bytes_accessed=4_000_000, transcendentals=250_000),
-    )(full, weight, norm_gain[None, :], proj, pick)
-    stats = lax.psum(stats, "space")
+        compiler_params=pltpu.CompilerParams(vmem_limit_bytes=40 * 1024 * 1024),
+        cost_estimate=pl.CostEstimate(
+            flops=4_000_000_000, bytes_accessed=4_000_000, transcendentals=1_000_000
+        ),
+    )(full, *rests)
 
     def to_owner(array):
         moved = lax.all_to_all(array, "tm", split_axis=1, concat_axis=0, tiled=True)
         moved = moved.reshape(frames_total, ROWS, groups, array.shape[-1])
         return jnp.swapaxes(moved, 0, 1).reshape(ROWS, frames_total * groups, array.shape[-1])
 
-    time_both = to_owner(tiles)
-    late = jnp.einsum("sp,lpc->lsc", pick, stats[:, :, HALF:], preferred_element_type=F32)
-    time_stats = to_owner(late.astype(BF16))
-    spatial = call(
+    early = to_owner(tiles)
+    late = call(
         spatial_kernel,
-        jax.ShapeDtypeStruct((OWN_BLK, owners * slots, part), BF16),
+        jax.ShapeDtypeStruct((OWN_BLK, owners * slots, 2 * part), BF16),
         scan_scratch(patches, part),
-        600_000_000,
-        inner, stats[:, :, :HALF], pick, perm, inverse, spread, dt_wide[:2], bias[:2], rate[:2],
+        20_000_000_000,
+        inner, stats, gate, pick, perm, inverse, spread, dt_wide[:2], bias[:2], rate[:2],
         (skip[0] + skip[1])[None, :],
     )
-    time_spatial = to_owner(spatial)
+    late = to_owner(late)
 
     clip_start = jnp.cumsum(clip_len) - clip_len
     row_frame = jnp.arange(frames_total, dtype=jnp.int32)
@@ -362,17 +376,26 @@
     closed = jnp.stack([opens, closes], axis=1).astype(F32)
     closed = jnp.repeat(closed, groups, axis=0)
     rows = frames_total * groups
+    temporal = call(
+        functools.partial(temporal_kernel, frames_total, groups, part),
+        jax.ShapeDtypeStruct((rows, lanes_of(part)), F32),
+        scan_scratch(rows, part),
+        20_000_000_000,
+        early, closed, perm, spread, dt_wide[2:], bias[2:], rate[2:], (skip[2] + skip[3])[None, :],
+    )
     term = call(
-        functools.partial(temporal_kernel, frames_total, groups),
+        output_kernel,
         jax.ShapeDtypeStruct((ROWS, rows, width), BF16),
-        scan_scratch(rows, part),
-        600_000_000,
-        time_both, time_spatial, time_stats, closed, perm, inverse, spread, dt_wide[2:], bias[2:],
-        rate[2:], (skip[2] + skip[3])[None, :], out_weight,
+        [],
+        2_000_000_000,
+        temporal, late, perm, inverse, out_weight,
     )
     term = term.reshape(ROWS, owners, OWN_BLK, groups, width)
-    term = jnp.transpose(term, (0, 3, 2, 1, 4)).reshape(slots, frames_total * width)[:per_owner]
-    return lax.psum_scatter(term, "space", scatter_dimension=1, tiled=True)
+    term = jnp.transpose(term, (2, 1, 0, 3, 4)).reshape(frames_total, slots, width)[:, :per_owner]
+    term = term.reshape(spaces, frames_total // spaces, per_owner, width)
+    term = lax.all_to_all(term, "space", split_axis=0, concat_axis=0, tiled=True)
+    mixed = jnp.sum(term.astype(F32), axis=0).astype(BF16)
+    return jnp.swapaxes(mixed, 0, 1).reshape(per_owner, frames_total // spaces * width)
 
 
 def solution(mesh):

time: 230 us -> 151 us (0.66)
  waiting for transfers between devices: 89.2 us -> 3.85 us
  blocking collectives: 9.42 us -> 25 us
  between operations: 13.8 us -> 0.52 us
  Pallas kernels: 45.1 us -> 51.1 us
  matrix products: 7.1 us -> 3.1 us
    psum x1 -> x0, waiting for transfers between devices: 32.2 us -> none  [body(): stats = lax.psum(stats, 'space')]
    all_to_all x3 -> x2, waiting for transfers between devices: 33.5 us -> 3.84 us  [to_owner(): moved = lax.all_to_all(array, 'tm', split_axis=1, concat_axis=0, tiled=True)]
    reduce_scatter x1 -> x0, waiting for transfers between devices: 23.5 us -> none  [body(): return lax.psum_scatter(term, 'space', scatter_dimension=1, tiled=True)]
    all_to_all x0 -> x1, blocking collectives: none -> 16.5 us  [body(): lax.all_to_all(term, 'space', split_axis=0, concat_axis=0, tiled=True)]
    ppermute x0 -> x3, starting transfers between devices: none -> 4.45 us  [body(): lax.ppermute(proj, 'space', [(i, (i + k) % spaces) for i in range(spaces)])]
    all_to_all x3 -> x2, starting transfers between devices: 13.2 us -> 9.54 us  [to_owner(): moved = lax.all_to_all(array, 'tm', split_axis=1, concat_axis=0, tiled=True)]
    pallas_call x1, Pallas kernels: 3.51 us -> 6.58 us  [body(): pl.pallas_call(first_kernel, grid=(OWN_BLK,), out_shape=(jax.ShapeDtypeSt...]
    pallas_call x2 -> x3, Pallas kernels: 41.6 us -> 44.5 us  [call(): pl.pallas_call(kernel, out_shape=out_shape, in_specs=[pl.BlockSpec(memory...]
  transfers between devices with their start and end apart: 6 -> 6, of which waited for: 4 -> 2; matrix products, arithmetic and copies ran while one was open for 13% -> 18% of each run, Pallas kernels for 8% -> 26%
where the time goes in v1:
time: 151 us; the launch traced here: 150 us
  Pallas kernels  51.1 us (34%)
  local copies, waits for them, and re-layouts  39.8 us (26%)
  blocking collectives  25 us (17%)
  starting transfers between devices  18.9 us (13%)
  other arithmetic  7.55 us (5%)
  waiting for transfers between devices  3.85 us (3%)
  matrix products  3.1 us (2%)
    pallas_call x3, Pallas kernels, call(): pl.pallas_call(kernel, out_shape=out_shape, in_specs=[pl.BlockSpec(memory...  44.5 us
    all_to_all x1, blocking collectives, body(): lax.all_to_all(term, 'space', split_axis=0, concat_axis=0, tiled=True)  16.5 us
    all_to_all x2, starting transfers between devices, to_owner(): moved = lax.all_to_all(array, 'tm', split_axis=1, concat_axis=0, tiled=True)  9.54 us
    all_gather x1, blocking collectives, body(): lax.all_gather(owned, 'space', axis=1, tiled=True)  8.48 us
    pallas_call x1, Pallas kernels, body(): pl.pallas_call(first_kernel, grid=(OWN_BLK,), out_shape=(jax.ShapeDtypeSt...  6.58 us
    unnamed x33, local copies, waits for them, and re-layouts  6.41 us
    all_to_all x1, starting transfers between devices, body(): lax.all_to_all(packed, 'tm', split_axis=0, concat_axis=0, tiled=True)  4.87 us
    ppermute x3, starting transfers between devices, body(): lax.ppermute(proj, 'space', [(i, (i + k) % spaces) for i in range(spaces)])  4.45 us
  transfers between devices with their start and end apart: 6, of which 2 were waited for; matrix products, arithmetic and copies ran while one was open for 18% of the time, Pallas kernels for 26%

profile of v1, /device:TPU:0, one launch (start us, length us, event | category | flops | bytes accessed | tf_op | source)
XLA Modules:
  0.0 149.8 jit_solution(5209740298611959689)
XLA Ops:
  0.0 1.3 fusion.23
  1.3 1.3 fusion.22
  2.7 0.5 concatenate.3
  3.2 0.5 collective-permute-start
  3.7 2.6 %collective-permute-start.1 = (bf16[288,272]{0,1:T(8,128)(2,1)S(1)}, bf16[288,272]{0,1:T(8,128)(2,1)}, u32[]{:S(2)}, u32[]{:S(2)}) collective-permute-start(bf16[288,272]{0,1:T(8,128)(2,1)S(1)} %concatenate.3), channel_id=1, source_target_pairs={{0,2},{1,3},{2,0},{3,1},{4,6},{5,7},{6,4},{7,5},{8,10},{9,11},{10,... | collective-permute-start | bytes 470024 | tf_op jit(solution)/shard_map/ppermute | solution.py:300
  6.2 1.4 collective-permute-start.2
  7.8 0.6 dynamic_slice.6
  8.4 0.7 and_select_fusion.7
  9.3 0.8 gather_fusion.1
  10.4 1.2 broadcast_select_fusion.1
  11.6 4.9 %all-to-all-start = ((bf16[4,2,28224]{2,1,0:T(2,128)(2,1)}), bf16[4,2,28224]{2,1,0:T(2,128)(2,1)}, u32[]{:S(2)}, u32[]{:S(2)}) async-start(bf16[4,2,28224]{2,1,0:T(2,128)(2,1)} %broadcast_select_fusion.1), calls=%async_computation | async-start | bytes 905216 | tf_op jit(solution)/shard_map/all_to_all | solution.py:316
  16.7 0.6 gather_fusion
  17.5 0.4 fusion
  18.0 0.6 broadcast_select_fusion
  18.6 0.9 fusion.20
  19.5 0.4 copy-done.6
  19.9 1.1 fusion.25
  21.1 0.7 fusion.21
  21.8 0.8 convolution_bitcast_fusion.1
  22.6 0.8 convolution_bitcast_fusion
  23.4 0.6 slice_add_fusion
  24.2 1.6 %constant_dynamic-slice_fusion.w_ref = bf16[2,576,288]{2,1,0:T(8,128)(2,1)S(1)} fusion(bf16[2,576,1152]{2,1,0:T(8,128)(2,1)} %all_ref.1, s32[]{:T(128)S(6)} %select_n.207), kind=kLoop, calls=%fused_computation.109 | loop fusion | bytes 1327108 | tf_op jit(solution)/shard_map/dynamic_slice | solution.py:279
  26.5 0.9 copy.104.dt_ref
  27.4 0.6 slice.87.bias_ref
  28.1 0.8 copy.101.closed_ref
  28.9 0.9 copy.102.dt_ref
  29.9 0.6 copy.103.bias_ref
  30.5 1.2 pad_maximum_fusion
  31.7 0.7 gather_fusion.3
  32.4 1.3 copy.93
  33.8 1.4 bitcast_select_fusion.proj_ref
  35.2 1.3 all_to_all.32
  36.5 0.8 gather_fusion.2
  37.4 8.5 %all-gather = bf16[4,28224,4]{1,2,0:T(4,128)(2,1)S(1)} all-gather(bf16[1,28224,4]{1,2,0:T(4,128)(2,1)S(1)} %select_bitcast_fusion), channel_id=1, replica_groups=mesh['groups'=2,'tm'=4,'space'=4] {'space'}, dimensions={0}, use_global_device_ids=true | all-gather | bytes 1128960 | tf_op jit(solution)/shard_map/all_gather | solution.py:321
  46.3 1.8 %reshape.508 = bf16[112896,4]{0,1:T(4,128)(2,1)} reshape(bf16[4,28224,4]{1,0,2:T(4,128)(2,1)S(1)} %copy.84) | data formatting | bytes 1806336
  48.1 2.0 %reshape.461.x_ref = bf16[4,196,576]{2,1,0:T(8,128)(2,1)S(1)} reshape(bf16[4,112896]{1,0:T(4,128)(2,1)} %bitcast.116) | data formatting | bytes 1806336 | tf_op jit(solution)/shard_map/reshape | solution.py:321
  50.1 1.7 %copy-done.1 = bf16[2,576,1152]{2,1,0:T(8,128)(2,1)S(1)} copy-done((bf16[2,576,1152]{2,1,0:T(8,128)(2,1)S(1)}, bf16[2,576,1152]{2,1,0:T(8,128)(2,1)}, u32[]{:S(2)}) %copy-start.1) | copy-done | bytes 2654232
  51.9 6.6 %shard_map.154 = (bf16[4,196,288]{2,1,0:T(8,128)(2,1)S(1)}, bf16[4,196,136]{2,1,0:T(8,128)(2,1)S(1)}, bf16[4,208,424]{2,1,0:T(8,128)(2,1)S(1)}, bf16[4,208,288]{2,1,0:T(8,128)(2,1)S(1)}) custom-call(bf16[4,196,576]{2,1,0:T(8,128)(2,1)S(1)} %reshape.461.x_ref, bf16[2,576,288]{2,1,0:T(8,128)(2,1)S(1)} %constant_dynamic-slice_fusion.w_ref, ...), custom_call_target="tpu_custom_call" | custom-call | flops 4000000000 | bytes 4000000 | tf_op jit(solution)/shard_map/pallas_call | solution.py:330
  58.5 0.8 copy-done.3
  59.3 0.8 copy-done.4
  60.2 0.8 copy-done.5
  60.9 1.6 %copy.95 = bf16[4,208,424]{2,0,1:T(4,128)(2,1)} copy(bf16[4,208,424]{2,1,0:T(8,128)(2,1)S(1)} %get-tuple-element.9) | data formatting | bytes 1411072 | tf_op jit(solution)/shard_map/pallas_call | solution.py:330
  62.5 5.1 %all-to-all-start.1 = ((bf16[4,208,424]{2,0,1:T(4,128)(2,1)}), bf16[4,208,424]{2,0,1:T(4,128)(2,1)S(1)}, u32[]{:S(2)}, u32[]{:S(2)}) async-start(bf16[4,208,424]{2,0,1:T(4,128)(2,1)} %copy.95), calls=%async_computation.1 | async-start | bytes 1703936 | tf_op jit(solution)/shard_map/all_to_all | solution.py:355
  67.6 18.7 %shard_map.156 = bf16[4,208,576]{2,1,0:T(8,128)(2,1)} custom-call(bf16[4,196,288]{2,1,0:T(8,128)(2,1)} %copy-done.4, bf16[4,196,136]{2,1,0:T(8,128)(2,1)} %copy-done.5, bf16[4,208,288]{2,1,0:T(8,128)(2,1)} %copy-done.3, bf16[208,196]{1,0:T(8,128)(2,1)} %copy-done.2, bf16[512,512]{1,0:T(8,128)(2,1)} %constant.174.clone.perm_ref.inverse_ref, ...), custom_call_target="tpu_custom_call" | custom-call | flops 20000000000 | bytes 8000000 | tf_op jit(solution)/shard_map/pallas_call | solution.py:253
  86.3 2.6 %copy.105 = bf16[4,208,576]{2,0,1:T(4,128)(2,1)} copy(bf16[4,208,576]{2,1,0:T(8,128)(2,1)} %shard_map.156) | data formatting | bytes 1916928 | tf_op jit(solution)/shard_map/pallas_call | solution.py:253
  88.9 0.7 all-to-all-done.1
  89.6 4.4 %all-to-all-start.2 = ((bf16[4,208,576]{2,0,1:T(4,128)(2,1)}), bf16[4,208,576]{2,0,1:T(4,128)(2,1)S(1)}, u32[]{:S(2)}, u32[]{:S(2)}) async-start(bf16[4,208,576]{2,0,1:T(4,128)(2,1)} %copy.105), calls=%async_computation.2 | async-start | bytes 2129920 | tf_op jit(solution)/shard_map/all_to_all | solution.py:355
  94.0 0.5 copy.96
  94.5 0.5 reshape.464
  95.0 0.7 copy.97
  95.6 1.1 copy.100.moved_ref
  96.7 20.2 %shard_map.155.temporal_ref = f32[208,1152]{1,0:T(8,128)} custom-call(bf16[4,208,424]{2,1,0:T(8,128)(2,1)} %copy.100.moved_ref, f32[208,2]{1,0:T(8,128)} %copy.101.closed_ref, bf16[512,512]{1,0:T(8,128)(2,1)} %constant.174.clone.perm_ref.inverse_ref, bf16[64,2048]{1,0:T(8,128)(2,1)} %constant.175.clone.spread_ref, bf16[2,144,1152]{2,1,0:T(8,128)(2,1)} %copy.102.dt_ref, ...), custom_call_target="tpu_custom_call" | custom-call | flops 20000000000 | bytes 8000000 | tf_op jit(solution)/shard_map/pallas_call | solution.py:253
  116.9 3.2 %all-to-all-done.2 = bf16[4,208,576]{2,0,1:T(4,128)(2,1)S(1)} async-done(((bf16[4,208,576]{2,0,1:T(4,128)(2,1)}), bf16[4,208,576]{2,0,1:T(4,128)(2,1)S(1)}, u32[]{:S(2)}, u32[]{:S(2)}) %all-to-all-start.2) | async-done | bytes 958496 | tf_op jit(solution)/shard_map/all_to_all | solution.py:355
  120.1 0.4 copy.106
  120.4 0.6 reshape.469
  121.0 0.4 copy.107
  121.4 1.1 copy.108.moved_ref
  122.6 5.6 %shard_map.157 = bf16[4,208,576]{2,1,0:T(8,128)(2,1)} custom-call(f32[208,1152]{1,0:T(8,128)} %shard_map.155.temporal_ref, bf16[4,208,576]{2,1,0:T(8,128)(2,1)} %copy.108.moved_ref, bf16[512,512]{1,0:T(8,128)(2,1)} %constant.174.clone.perm_ref.inverse_ref, bf16[512,512]{1,0:T(8,128)(2,1)} %constant.174.clone.perm_ref.inverse_ref, bf16[288,576]{1,0:T(8,128)(2,1)} %w_ref.1), custom_call_target="tpu_custom_call" | custom-call | flops 2000000000 | bytes 8000000 | tf_op jit(solution)/shard_map/pallas_call | solution.py:253
  128.2 1.6 %copy.109 = bf16[4,208,576]{2,0,1:T(4,128)(2,1)S(1)} copy(bf16[4,208,576]{2,1,0:T(8,128)(2,1)} %shard_map.157) | data formatting | bytes 1916928 | tf_op jit(solution)/shard_map/pallas_call | solution.py:253
  129.8 0.4 copy.110
  130.2 0.6 reshape.472
  131.5 16.5 %all_to_all.44 = bf16[4,4,49,576]{3,1,2,0:T(4,128)(2,1)S(1)} all-to-all(bf16[4,4,49,576]{3,1,2,0:T(4,128)(2,1)S(1)} %copy.111), channel_id=1, replica_groups=mesh['groups'=2,'tm'=4,'space'=4] {'space'}, dimensions={0} | all-to-all | bytes 1806336 | tf_op jit(solution)/shard_map/all_to_all | solution.py:396
  148.1 0.7 reduce_sum.22
  148.8 1.0 reshape.474
  (79 shorter events, 3.3 us)
Async XLA Ops:
  0.0 9.3 %copy-start = (bf16[8,28224]{1,0:T(8,128)(2,1)S(1)}, bf16[8,28224]{1,0:T(8,128)(2,1)}, u32[]{:S(2)}) copy-start(bf16[8,28224]{1,0:T(8,128)(2,1)} %param.16) | copy-start | bytes 1354756
  0.0 7.6 %copy-start.12 = (s32[4]{0:T(128)S(1)}, s32[4]{0:T(128)}, u32[]{:S(2)}) copy-start(s32[4]{0:T(128)} %param.17) | copy-start | bytes 52
  3.2 27.3 %collective-permute-start = (bf16[288,272]{0,1:T(8,128)(2,1)S(1)}, bf16[288,272]{0,1:T(8,128)(2,1)S(1)}, u32[]{:S(2)}, u32[]{:S(2)}) collective-permute-start(bf16[288,272]{0,1:T(8,128)(2,1)S(1)} %concatenate.3), channel_id=1, source_target_pairs={{0,1},{1,2},{2,3},{3,0},{4,5},{5,6},{6,7},{7,4},{8,9},{9,10},{10,1... | collective-permute-start | bytes 470024 | tf_op jit(solution)/shard_map/ppermute | solution.py:300
  3.7 26.8 %collective-permute-start.1 = (bf16[288,272]{0,1:T(8,128)(2,1)S(1)}, bf16[288,272]{0,1:T(8,128)(2,1)}, u32[]{:S(2)}, u32[]{:S(2)}) collective-permute-start(bf16[288,272]{0,1:T(8,128)(2,1)S(1)} %concatenate.3), channel_id=1, source_target_pairs={{0,2},{1,3},{2,0},{3,1},{4,6},{5,7},{6,4},{7,5},{8,10},{9,11},{10,... | collective-permute-start | bytes 470024 | tf_op jit(solution)/shard_map/ppermute | solution.py:300
  6.2 24.2 %collective-permute-start.2 = (bf16[288,272]{0,1:T(8,128)(2,1)S(1)}, bf16[288,272]{0,1:T(8,128)(2,1)}, u32[]{:S(2)}, u32[]{:S(2)}) collective-permute-start(bf16[288,272]{0,1:T(8,128)(2,1)S(1)} %concatenate.3), channel_id=1, source_target_pairs={{0,3},{1,0},{2,1},{3,2},{4,7},{5,4},{6,5},{7,6},{8,11},{9,8},{10,9... | collective-permute-start | bytes 470024 | tf_op jit(solution)/shard_map/ppermute | solution.py:300
  10.3 7.1 %copy-start.7 = (s32[196,196]{1,0:T(8,128)S(1)}, s32[196,196]{1,0:T(8,128)}, u32[]{:S(2)}) copy-start(s32[196,196]{1,0:T(8,128)} %param.19) | copy-start | bytes 460996
  10.4 7.1 %copy-start.14 = (bf16[4,36,288]{2,0,1:T(4,128)(2,1)S(1)}, bf16[4,36,288]{2,0,1:T(4,128)(2,1)}, u32[]{:S(2)}) copy-start(bf16[4,36,288]{2,0,1:T(4,128)(2,1)} %param.23) | copy-start | bytes 248836
  10.4 7.1 %copy-start.15 = (bf16[288,1152,1]{1,0,2:T(8,128)(2,1)S(1)}, bf16[288,1152,1]{1,0,2:T(8,128)(2,1)}, u32[]{:S(2)}) copy-start(bf16[288,1152,1]{1,0,2:T(8,128)(2,1)} %constant.179) | copy-start | bytes 1990660
  11.6 23.6 %all-to-all-start = ((bf16[4,2,28224]{2,1,0:T(2,128)(2,1)}), bf16[4,2,28224]{2,1,0:T(2,128)(2,1)}, u32[]{:S(2)}, u32[]{:S(2)}) async-start(bf16[4,2,28224]{2,1,0:T(2,128)(2,1)} %broadcast_select_fusion.1), calls=%async_computation | async-start | bytes 905216 | tf_op jit(solution)/shard_map/all_to_all | solution.py:316
  18.6 1.3 copy-start.6
  18.6 1.3 copy-start.8
  19.9 1.9 %copy-start.9 = (f32[4,288]{1,0:T(4,128)S(1)}, f32[4,288]{1,0:T(4,128)}, u32[]{:S(2)}) copy-start(f32[4,288]{1,0:T(4,128)} %param.24) | copy-start | bytes 13828
  21.1 1.6 %copy-start.10 = (f32[4,288]{1,0:T(4,128)S(1)}, f32[4,288]{1,0:T(4,128)}, u32[]{:S(2)}) copy-start(f32[4,288]{1,0:T(4,128)} %param.26) | copy-start | bytes 13828
  21.8 2.2 %copy-start.13 = (s32[4]{0:T(128)S(1)}, s32[4]{0:T(128)}, u32[]{:S(2)}) copy-start(s32[4]{0:T(128)} %param.18) | copy-start | bytes 52
  24.2 2.2 %copy-start.11 = (f32[576]{0:T(1024)S(1)}, f32[576]{0:T(1024)}, u32[]{:S(2)}) copy-start(f32[576]{0:T(1024)} %param.20) | copy-start | bytes 6916
  26.4 23.7 %copy-start.2 = (bf16[208,196]{1,0:T(8,128)(2,1)}, bf16[208,196]{1,0:T(8,128)(2,1)S(1)}, u32[]{:S(2)}) copy-start(bf16[208,196]{1,0:T(8,128)(2,1)S(1)} %reshape.463.pick_ref) | copy-start | bytes 244612
  50.1 1.8 %copy-start.1 = (bf16[2,576,1152]{2,1,0:T(8,128)(2,1)S(1)}, bf16[2,576,1152]{2,1,0:T(8,128)(2,1)}, u32[]{:S(2)}) copy-start(bf16[2,576,1152]{2,1,0:T(8,128)(2,1)} %all_ref.1) | copy-start | bytes 7962628
  58.5 0.9 copy-start.3
  59.3 0.8 copy-start.4
  60.2 0.8 copy-start.5
  62.5 27.1 %all-to-all-start.1 = ((bf16[4,208,424]{2,0,1:T(4,128)(2,1)}), bf16[4,208,424]{2,0,1:T(4,128)(2,1)S(1)}, u32[]{:S(2)}, u32[]{:S(2)}) async-start(bf16[4,208,424]{2,0,1:T(4,128)(2,1)} %copy.95), calls=%async_computation.1 | async-start | bytes 1703936 | tf_op jit(solution)/shard_map/all_to_all | solution.py:355
  89.6 30.5 %all-to-all-start.2 = ((bf16[4,208,576]{2,0,1:T(4,128)(2,1)}), bf16[4,208,576]{2,0,1:T(4,128)(2,1)S(1)}, u32[]{:S(2)}, u32[]{:S(2)}) async-start(bf16[4,208,576]{2,0,1:T(4,128)(2,1)} %copy.105), calls=%async_computation.2 | async-start | bytes 2129920 | tf_op jit(solution)/shard_map/all_to_all | solution.py:355

commit v2 on v1

--- a/solution.py
+++ b/solution.py
@@ -290,35 +290,40 @@
     lane_row = (jnp.arange(lanes_of(part), dtype=jnp.int32) % 128) // 32
     same = (lane_row[None, :] == jnp.arange(ROWS, dtype=jnp.int32)[:, None])[None, :, None, :]
     dt_wide = jnp.where(same, dt_wide[:, None], jnp.zeros((), BF16)).reshape(4, ROWS * RANK, lanes_of(part))
+    pick = tile_pick.astype(BF16).T.reshape(owners, per_owner, patches)
+    pick = jnp.pad(pick, ((0, 0), (0, slots - per_owner), (0, 0))).reshape(owners * slots, patches)
+    perm, inverse = jnp.asarray(PERM, BF16), jnp.asarray(PERM.T, BF16)
+    spread = jnp.asarray(SPREAD, BF16)
+
+    capacity = (IN_BLK + owners - 1) // owners
+    offsets = jnp.cumsum(arrive_len) - arrive_len
+    lane_index = jnp.arange(capacity, dtype=jnp.int32)[None, :]
+    target_ids = jnp.arange(owners, dtype=jnp.int32)[:, None]
+    slot_index = (target_ids - offsets[my_owner]) % owners + lane_index * owners
+    packed = jnp.take(frames_in, jnp.minimum(slot_index, IN_BLK - 1).reshape(-1), axis=0)
+    packed, proj_weight = lax.optimization_barrier((packed, proj_weight))
+    arrived = lax.all_to_all(packed, "tm", split_axis=0, concat_axis=0, tiled=True)
     pieces = []
     for half in (0, 2):
         pieces += [proj_weight[half, :, :RANK], proj_weight[half + 1, :, :RANK]]
         pieces += [proj_weight[half, :, RANK:], proj_weight[half + 1, :, RANK:]]
     proj = jnp.concatenate(pieces, axis=1)
     spaces = lax.axis_size("space")
-    shares = [proj] + [
-        lax.ppermute(proj, "space", [(i, (i + k) % spaces) for i in range(spaces)])
-        for k in range(1, spaces)
-    ]
     order = (space_index - jnp.arange(spaces, dtype=jnp.int32)) % spaces
-    proj = jnp.take(jnp.stack(shares), order, axis=0).reshape(spaces * part, 2 * HALF)
-    pick = tile_pick.astype(BF16).T.reshape(owners, per_owner, patches)
-    pick = jnp.pad(pick, ((0, 0), (0, slots - per_owner), (0, 0))).reshape(owners * slots, patches)
-    perm, inverse = jnp.asarray(PERM, BF16), jnp.asarray(PERM.T, BF16)
-    spread = jnp.asarray(SPREAD, BF16)
-
-    capacity = (IN_BLK + owners - 1) // owners
-    offsets = jnp.cumsum(arrive_len) - arrive_len
-    lane_index = jnp.arange(capacity, dtype=jnp.int32)[None, :]
-    target_ids = jnp.arange(owners, dtype=jnp.int32)[:, None]
-    slot_index = (target_ids - offsets[my_owner]) % owners + lane_index * owners
-    packed = jnp.take(frames_in, jnp.minimum(slot_index, IN_BLK - 1).reshape(-1), axis=0)
-    arrived = lax.all_to_all(packed, "tm", split_axis=0, concat_axis=0, tiled=True)
+
+    def to_next(array, k):
+        return lax.ppermute(array, "space", [(i, (i + k) % spaces) for i in range(spaces)])
+
+    def gathered(array):
+        shares = [array] + [to_next(array, k) for k in range(1, spaces)]
+        return jnp.take(jnp.stack(shares), order, axis=0)
+
+    proj = gathered(proj).reshape(spaces * part, 2 * HALF)
     wanted = jnp.arange(OWN_BLK, dtype=jnp.int32) * owners + my_owner
     sender = jnp.sum((offsets[None, :] <= wanted[:, None]).astype(jnp.int32), axis=1) - 1
     lane_of = (wanted - offsets[sender]) // owners
     owned = jnp.take(arrived, sender * capacity + lane_of, axis=0)
-    full = lax.all_gather(owned, "space", axis=1, tiled=True).reshape(OWN_BLK, patches, width)
+    full = jnp.swapaxes(gathered(owned), 0, 1).reshape(OWN_BLK, patches, width)
 
     def per_frame(*dims):
         return pl.BlockSpec((1,) + dims, lambda i: (i, 0, 0))
@@ -393,8 +398,11 @@
     term = term.reshape(ROWS, owners, OWN_BLK, groups, width)
     term = jnp.transpose(term, (2, 1, 0, 3, 4)).reshape(frames_total, slots, width)[:, :per_owner]
     term = term.reshape(spaces, frames_total // spaces, per_owner, width)
-    term = lax.all_to_all(term, "space", split_axis=0, concat_axis=0, tiled=True)
-    mixed = jnp.sum(term.astype(F32), axis=0).astype(BF16)
+    mixed = 0.0
+    for k in range(spaces):
+        piece = lax.dynamic_index_in_dim(term, (space_index + k) % spaces, 0, keepdims=False)
+        mixed = mixed + (to_next(piece, k) if k else piece).astype(F32)
+    mixed = mixed.astype(BF16)
     return jnp.swapaxes(mixed, 0, 1).reshape(per_owner, frames_total // spaces * width)
 
 

time: 151 us -> 156 us (1.033)
  blocking collectives: 25 us -> 0 us
  waiting for transfers between devices: 3.85 us -> 24 us
  starting transfers between devices: 18.9 us -> 22.5 us
  local copies, waits for them, and re-layouts: 39.8 us -> 42.5 us
  other arithmetic: 7.55 us -> 9.91 us
    ppermute x3 -> x9, waiting for transfers between devices: 0.01 us -> 18.4 us  [to_next(): lax.ppermute(array, 'space', [(i, (i + k) % spaces) for i in range(spaces)])]
    all_to_all x1 -> x0, blocking collectives: 16.5 us -> none  [body(): lax.all_to_all(term, 'space', split_axis=0, concat_axis=0, tiled=True)]
    all_gather x1 -> x0, blocking collectives: 8.48 us -> none  [body(): lax.all_gather(owned, 'space', axis=1, tiled=True)]
    ppermute x3 -> x9, starting transfers between devices: 4.45 us -> 8.58 us  [to_next(): lax.ppermute(array, 'space', [(i, (i + k) % spaces) for i in range(spaces)])]
    slice x2 -> x0, local copies, waits for them, and re-layouts: 2.62 us -> none  [the longest x1 1.34 us: body(): pieces += [proj_weight[half, :, :RANK], proj_weight[half + 1, :, :RANK]]]
    gather x2 -> x3, local copies, waits for them, and re-layouts: 2.05 us -> 4.27 us  [gathered(): return jnp.take(jnp.stack(shares), order, axis=0)]
    all_to_all x2, waiting for transfers between devices: 3.84 us -> 5.67 us  [to_owner(): moved = lax.all_to_all(array, 'tm', split_axis=1, concat_axis=0, tiled=True)]
    unnamed x33 -> x32, local copies, waits for them, and re-layouts: 6.41 us -> 4.63 us
  transfers between devices with their start and end apart: 6 -> 12, of which waited for: 2 -> 8; matrix products, arithmetic and copies ran while one was open for 18% -> 15% of each run, Pallas kernels for 26% -> 25%
where the time goes in v2:
time: 156 us; the launch traced here: 154 us
  Pallas kernels  51.1 us (33%)
  local copies, waits for them, and re-layouts  42.5 us (27%)
  waiting for transfers between devices  24 us (15%)
  starting transfers between devices  22.5 us (14%)
  other arithmetic  9.91 us (6%)
  matrix products  3.1 us (2%)
    pallas_call x3, Pallas kernels, call(): pl.pallas_call(kernel, out_shape=out_shape, in_specs=[pl.BlockSpec(memory...  44.6 us
    ppermute x9, waiting for transfers between devices, to_next(): lax.ppermute(array, 'space', [(i, (i + k) % spaces) for i in range(spaces)])  18.4 us
    all_to_all x2, starting transfers between devices, to_owner(): moved = lax.all_to_all(array, 'tm', split_axis=1, concat_axis=0, tiled=True)  9.08 us
    ppermute x9, starting transfers between devices, to_next(): lax.ppermute(array, 'space', [(i, (i + k) % spaces) for i in range(spaces)])  8.58 us
    pallas_call x1, Pallas kernels, body(): pl.pallas_call(first_kernel, grid=(OWN_BLK,), out_shape=(jax.ShapeDtypeSt...  6.58 us
    all_to_all x2, waiting for transfers between devices, to_owner(): moved = lax.all_to_all(array, 'tm', split_axis=1, concat_axis=0, tiled=True)  5.67 us
    all_to_all x1, starting transfers between devices, body(): lax.all_to_all(packed, 'tm', split_axis=0, concat_axis=0, tiled=True)  4.87 us
    unnamed x32, local copies, waits for them, and re-layouts  4.63 us
  transfers between devices with their start and end apart: 12, of which 8 were waited for; matrix products, arithmetic and copies ran while one was open for 15% of the time, Pallas kernels for 25%

profile of v2, /device:TPU:0, one launch (start us, length us, event | category | flops | bytes accessed | tf_op | source)
XLA Modules:
  0.0 153.8 jit_solution(10698940903790989760)
XLA Ops:
  0.0 0.9 reduce-window.16
  0.9 0.7 bitcast_subtract_fusion.2
  1.5 0.6 dynamic_slice.19
  2.1 0.7 and_select_fusion.6
  3.1 0.8 gather_fusion.1
  5.2 2.6 %collective-permute-start.4 = (bf16[288,272]{0,1:T(8,128)(2,1)S(1)}, bf16[288,272]{0,1:T(8,128)(2,1)}, u32[]{:S(2)}, u32[]{:S(2)}) collective-permute-start(bf16[288,272]{0,1:T(8,128)(2,1)S(1)} %concatenate.3), channel_id=1, source_target_pairs={{0,2},{1,3},{2,0},{3,1},{4,6},{5,7},{6,4},{7,5},{8,10},{9,11},{10,... | collective-permute-start | bytes 470024 | tf_op jit(solution)/shard_map/ppermute | solution.py:315
  7.7 1.4 collective-permute-start.5
  9.1 0.9 all_to_all.30
  10.0 4.9 %all-to-all-start = ((bf16[4,2,28224]{2,1,0:T(2,128)(2,1)}), bf16[4,2,28224]{2,1,0:T(2,128)(2,1)}, u32[]{:S(2)}, u32[]{:S(2)}) async-start(bf16[4,2,28224]{2,1,0:T(2,128)(2,1)} %all_to_all.30), calls=%async_computation | async-start | bytes 905216 | tf_op jit(solution)/shard_map/all_to_all | solution.py:305
  15.1 0.6 gather_fusion
  17.0 0.9 fusion.24
  18.3 1.1 fusion.27
  19.5 0.7 fusion.25
  20.3 0.8 convolution_bitcast_fusion.1
  21.1 0.8 convolution_bitcast_fusion
  21.9 0.6 slice_add_fusion
  22.7 1.6 %constant_dynamic-slice_fusion.w_ref = bf16[2,576,288]{2,1,0:T(8,128)(2,1)S(1)} fusion(bf16[2,576,1152]{2,1,0:T(8,128)(2,1)} %all_ref.1, s32[]{:T(128)S(6)} %select_n.262), kind=kLoop, calls=%fused_computation.89 | loop fusion | bytes 1327108 | tf_op jit(solution)/shard_map/dynamic_slice | solution.py:279
  25.0 0.9 copy.102.dt_ref
  25.9 0.6 slice.87.bias_ref
  26.6 0.8 copy.99.closed_ref
  27.4 0.9 copy.100.dt_ref
  28.3 0.6 copy.101.bias_ref
  28.9 1.2 pad_maximum_fusion.1
  30.2 0.7 gather_fusion.4
  30.9 1.3 copy.91
  32.3 1.4 bitcast_select_fusion.proj_ref
  33.7 1.3 all_to_all.32
  35.0 0.8 gather_fusion.2
  36.0 0.6 collective-permute-start.1
  36.6 1.4 collective-permute-start.2
  38.2 5.0 %collective-permute-done = bf16[4,28224]{1,0:T(4,128)(2,1)S(1)} collective-permute-done((bf16[4,28224]{1,0:T(4,128)(2,1)S(1)}, bf16[4,28224]{1,0:T(4,128)(2,1)S(1)}, u32[]{:S(2)}, u32[]{:S(2)}) %collective-permute-start) | collective-permute-done | bytes 225824 | tf_op jit(solution)/shard_map/ppermute | solution.py:315
  43.2 1.2 collective-permute-done.1
  44.4 2.3 %collective-permute-done.2 = bf16[4,28224]{1,0:T(4,128)(2,1)S(1)} collective-permute-done((bf16[4,28224]{1,0:T(4,128)(2,1)S(1)}, bf16[4,28224]{1,0:T(4,128)(2,1)S(1)}, u32[]{:S(2)}, u32[]{:S(2)}) %collective-permute-start.2) | collective-permute-done | bytes 225824 | tf_op jit(solution)/shard_map/ppermute | solution.py:315
  46.7 0.8 pad_maximum_fusion
  47.6 2.2 %gather_fusion.3 = bf16[4,4,28224]{2,1,0:T(4,128)(2,1)} fusion(bf16[4,4,28224]{2,1,0:T(4,128)(2,1)S(1)} %pad_maximum_fusion, s32[1024]{0:T(1024)S(1)} %pad_clamp_fusion), kind=kCustom, calls=%fused_computation.3 | custom fusion | bytes 1806352 | tf_op jit(solution)/shard_map/jit(_take)/gather | solution.py:319
  49.8 1.6 %select_bitcast_fusion = bf16[4,4,28224]{2,0,1:T(4,128)(2,1)S(1)} fusion(bf16[4,4,28224]{2,1,0:T(4,128)(2,1)} %gather_fusion.3, pred[4]{0:T(512)(128)(4,1)S(1)} %compare_and_fusion.2), kind=kLoop, calls=%fused_computation.11 | loop fusion | flops 451584 | bytes 1806340 | tf_op jit(solution)/shard_map/jit(_take)/select_n | solution.py:319
  51.4 1.3 copy.82
  52.7 2.6 %reshape.484.x_ref = bf16[4,196,576]{2,1,0:T(8,128)(2,1)S(1)} reshape(bf16[4,4,28224]{2,1,0:T(4,128)(2,1)} %copy.82) | data formatting | bytes 1806336 | tf_op jit(solution)/shard_map/reshape | solution.py:326
  55.3 1.7 %copy-done.1 = bf16[2,576,1152]{2,1,0:T(8,128)(2,1)S(1)} copy-done((bf16[2,576,1152]{2,1,0:T(8,128)(2,1)S(1)}, bf16[2,576,1152]{2,1,0:T(8,128)(2,1)}, u32[]{:S(2)}) %copy-start.1) | copy-done | bytes 2654232
  57.1 6.6 %shard_map.154 = (bf16[4,196,288]{2,1,0:T(8,128)(2,1)S(1)}, bf16[4,196,136]{2,1,0:T(8,128)(2,1)S(1)}, bf16[4,208,424]{2,1,0:T(8,128)(2,1)S(1)}, bf16[4,208,288]{2,1,0:T(8,128)(2,1)S(1)}) custom-call(bf16[4,196,576]{2,1,0:T(8,128)(2,1)S(1)} %reshape.484.x_ref, bf16[2,576,288]{2,1,0:T(8,128)(2,1)S(1)} %constant_dynamic-slice_fusion.w_ref, ...), custom_call_target="tpu_custom_call" | custom-call | flops 4000000000 | bytes 4000000 | tf_op jit(solution)/shard_map/pallas_call | solution.py:335
  63.7 0.8 copy-done.3
  64.5 0.8 copy-done.4
  65.3 0.8 copy-done.5
  66.1 1.6 %copy.93 = bf16[4,208,424]{2,0,1:T(4,128)(2,1)} copy(bf16[4,208,424]{2,1,0:T(8,128)(2,1)S(1)} %get-tuple-element.13) | data formatting | bytes 1411072 | tf_op jit(solution)/shard_map/pallas_call | solution.py:335
  67.7 5.1 %all-to-all-start.1 = ((bf16[4,208,424]{2,0,1:T(4,128)(2,1)}), bf16[4,208,424]{2,0,1:T(4,128)(2,1)S(1)}, u32[]{:S(2)}, u32[]{:S(2)}) async-start(bf16[4,208,424]{2,0,1:T(4,128)(2,1)} %copy.93), calls=%async_computation.1 | async-start | bytes 1703936 | tf_op jit(solution)/shard_map/all_to_all | solution.py:360
  72.8 18.7 %shard_map.156 = bf16[4,208,576]{2,1,0:T(8,128)(2,1)} custom-call(bf16[4,196,288]{2,1,0:T(8,128)(2,1)} %copy-done.4, bf16[4,196,136]{2,1,0:T(8,128)(2,1)} %copy-done.5, bf16[4,208,288]{2,1,0:T(8,128)(2,1)} %copy-done.3, bf16[208,196]{1,0:T(8,128)(2,1)} %copy-done.2, bf16[512,512]{1,0:T(8,128)(2,1)} %constant.215.clone.perm_ref.inverse_ref, ...), custom_call_target="tpu_custom_call" | custom-call | flops 20000000000 | bytes 8000000 | tf_op jit(solution)/shard_map/pallas_call | solution.py:253
  91.5 2.7 %copy.103 = bf16[4,208,576]{2,0,1:T(4,128)(2,1)} copy(bf16[4,208,576]{2,1,0:T(8,128)(2,1)} %shard_map.156) | data formatting | bytes 1916928 | tf_op jit(solution)/shard_map/pallas_call | solution.py:253
  94.1 1.1 all-to-all-done.1
  95.3 4.0 %all-to-all-start.2 = ((bf16[4,208,576]{2,0,1:T(4,128)(2,1)}), bf16[4,208,576]{2,0,1:T(4,128)(2,1)S(1)}, u32[]{:S(2)}, u32[]{:S(2)}) async-start(bf16[4,208,576]{2,0,1:T(4,128)(2,1)} %copy.103), calls=%async_computation.2 | async-start | bytes 2129920 | tf_op jit(solution)/shard_map/all_to_all | solution.py:360
  100.2 0.7 copy.95
  100.8 1.1 copy.98.moved_ref
  101.9 20.2 %shard_map.155.temporal_ref = f32[208,1152]{1,0:T(8,128)} custom-call(bf16[4,208,424]{2,1,0:T(8,128)(2,1)} %copy.98.moved_ref, f32[208,2]{1,0:T(8,128)} %copy.99.closed_ref, bf16[512,512]{1,0:T(8,128)(2,1)} %constant.215.clone.perm_ref.inverse_ref, bf16[64,2048]{1,0:T(8,128)(2,1)} %constant.216.clone.spread_ref, bf16[2,144,1152]{2,1,0:T(8,128)(2,1)} %copy.100.dt_ref, ...), custom_call_target="tpu_custom_call" | custom-call | flops 20000000000 | bytes 8000000 | tf_op jit(solution)/shard_map/pallas_call | solution.py:253
  122.1 4.6 %all-to-all-done.2 = bf16[4,208,576]{2,0,1:T(4,128)(2,1)S(1)} async-done(((bf16[4,208,576]{2,0,1:T(4,128)(2,1)}), bf16[4,208,576]{2,0,1:T(4,128)(2,1)S(1)}, u32[]{:S(2)}, u32[]{:S(2)}) %all-to-all-start.2) | async-done | bytes 958496 | tf_op jit(solution)/shard_map/all_to_all | solution.py:360
  128.0 1.1 copy.106.moved_ref
  129.2 5.6 %shard_map.157 = bf16[4,208,576]{2,1,0:T(8,128)(2,1)} custom-call(f32[208,1152]{1,0:T(8,128)} %shard_map.155.temporal_ref, bf16[4,208,576]{2,1,0:T(8,128)(2,1)} %copy.106.moved_ref, bf16[512,512]{1,0:T(8,128)(2,1)} %constant.215.clone.perm_ref.inverse_ref, bf16[512,512]{1,0:T(8,128)(2,1)} %constant.215.clone.perm_ref.inverse_ref, bf16[288,576]{1,0:T(8,128)(2,1)} %w_ref.1), custom_call_target="tpu_custom_call" | custom-call | flops 2000000000 | bytes 8000000 | tf_op jit(solution)/shard_map/pallas_call | solution.py:253
  134.8 1.6 %copy.107 = bf16[4,208,576]{2,0,1:T(4,128)(2,1)S(1)} copy(bf16[4,208,576]{2,1,0:T(8,128)(2,1)} %shard_map.157) | data formatting | bytes 1916928 | tf_op jit(solution)/shard_map/pallas_call | solution.py:253
  137.4 1.1 slice.120
  138.5 1.8 %reshape.496 = bf16[4,4,49,576]{3,1,0,2:T(4,128)(2,1)S(1)} reshape(bf16[16,49,576]{2,0,1:T(8,128)(2,1)} %slice.120) | data formatting | bytes 1806336 | tf_op jit(solution)/shard_map/reshape | solution.py:400
  140.7 0.6 collective-permute-start.7
  141.3 1.4 collective-permute-start.8
  142.7 5.7 %collective-permute-done.6 = bf16[4,49,576]{2,0,1:T(4,128)(2,1)S(1)} collective-permute-done((bf16[4,49,576]{2,0,1:T(4,128)(2,1)S(1)}, bf16[4,49,576]{2,0,1:T(4,128)(2,1)S(1)}, u32[]{:S(2)}, u32[]{:S(2)}) %collective-permute-start.6) | collective-permute-done | bytes 225824 | tf_op jit(solution)/shard_map/ppermute | solution.py:315
  148.4 1.2 collective-permute-done.7
  149.7 2.8 %collective-permute-done.8 = bf16[4,49,576]{2,0,1:T(4,128)(2,1)S(1)} collective-permute-done((bf16[4,49,576]{2,0,1:T(4,128)(2,1)S(1)}, bf16[4,49,576]{2,0,1:T(4,128)(2,1)S(1)}, u32[]{:S(2)}, u32[]{:S(2)}) %collective-permute-start.8) | collective-permute-done | bytes 225824 | tf_op jit(solution)/shard_map/ppermute | solution.py:315
  152.8 1.0 reshape.497
  (90 shorter events, 8.4 us)
Async XLA Ops:
  0.0 3.1 %copy-start = (bf16[8,28224]{1,0:T(8,128)(2,1)S(1)}, bf16[8,28224]{1,0:T(8,128)(2,1)}, u32[]{:S(2)}) copy-start(bf16[8,28224]{1,0:T(8,128)(2,1)} %param.16) | copy-start | bytes 1354756
  3.1 1.0 copy-start.7
  4.2 11.7 %copy-start.8 = (s32[196,196]{1,0:T(8,128)S(1)}, s32[196,196]{1,0:T(8,128)}, u32[]{:S(2)}) copy-start(s32[196,196]{1,0:T(8,128)} %param.19) | copy-start | bytes 460996
  4.6 11.3 %copy-start.14 = (bf16[4,36,288]{2,0,1:T(4,128)(2,1)S(1)}, bf16[4,36,288]{2,0,1:T(4,128)(2,1)}, u32[]{:S(2)}) copy-start(bf16[4,36,288]{2,0,1:T(4,128)(2,1)} %param.23) | copy-start | bytes 248836
  4.6 11.3 %copy-start.15 = (bf16[288,1152,1]{1,0,2:T(8,128)(2,1)S(1)}, bf16[288,1152,1]{1,0,2:T(8,128)(2,1)}, u32[]{:S(2)}) copy-start(bf16[288,1152,1]{1,0,2:T(8,128)(2,1)} %constant.220) | copy-start | bytes 1990660
  4.7 24.3 %collective-permute-start.3 = (bf16[288,272]{0,1:T(8,128)(2,1)S(1)}, bf16[288,272]{0,1:T(8,128)(2,1)S(1)}, u32[]{:S(2)}, u32[]{:S(2)}) collective-permute-start(bf16[288,272]{0,1:T(8,128)(2,1)S(1)} %concatenate.3), channel_id=1, source_target_pairs={{0,1},{1,2},{2,3},{3,0},{4,5},{5,6},{6,7},{7,4},{8,9},{9,10},{10,1... | collective-permute-start | bytes 470024 | tf_op jit(solution)/shard_map/ppermute | solution.py:315
  5.2 23.8 %collective-permute-start.4 = (bf16[288,272]{0,1:T(8,128)(2,1)S(1)}, bf16[288,272]{0,1:T(8,128)(2,1)}, u32[]{:S(2)}, u32[]{:S(2)}) collective-permute-start(bf16[288,272]{0,1:T(8,128)(2,1)S(1)} %concatenate.3), channel_id=1, source_target_pairs={{0,2},{1,3},{2,0},{3,1},{4,6},{5,7},{6,4},{7,5},{8,10},{9,11},{10,... | collective-permute-start | bytes 470024 | tf_op jit(solution)/shard_map/ppermute | solution.py:315
  7.7 21.2 %collective-permute-start.5 = (bf16[288,272]{0,1:T(8,128)(2,1)S(1)}, bf16[288,272]{0,1:T(8,128)(2,1)}, u32[]{:S(2)}, u32[]{:S(2)}) collective-permute-start(bf16[288,272]{0,1:T(8,128)(2,1)S(1)} %concatenate.3), channel_id=1, source_target_pairs={{0,3},{1,0},{2,1},{3,2},{4,7},{5,4},{6,5},{7,6},{8,11},{9,8},{10,9... | collective-permute-start | bytes 470024 | tf_op jit(solution)/shard_map/ppermute | solution.py:315
  10.0 23.6 %all-to-all-start = ((bf16[4,2,28224]{2,1,0:T(2,128)(2,1)}), bf16[4,2,28224]{2,1,0:T(2,128)(2,1)}, u32[]{:S(2)}, u32[]{:S(2)}) async-start(bf16[4,2,28224]{2,1,0:T(2,128)(2,1)} %all_to_all.30), calls=%async_computation | async-start | bytes 905216 | tf_op jit(solution)/shard_map/all_to_all | solution.py:305
  17.0 1.3 copy-start.6
  17.0 1.3 copy-start.9
  18.3 1.9 %copy-start.10 = (f32[4,288]{1,0:T(4,128)S(1)}, f32[4,288]{1,0:T(4,128)}, u32[]{:S(2)}) copy-start(f32[4,288]{1,0:T(4,128)} %param.24) | copy-start | bytes 13828
  19.5 1.6 %copy-start.11 = (f32[4,288]{1,0:T(4,128)S(1)}, f32[4,288]{1,0:T(4,128)}, u32[]{:S(2)}) copy-start(f32[4,288]{1,0:T(4,128)} %param.26) | copy-start | bytes 13828
  20.3 2.2 %copy-start.13 = (s32[4]{0:T(128)S(1)}, s32[4]{0:T(128)}, u32[]{:S(2)}) copy-start(s32[4]{0:T(128)} %param.18) | copy-start | bytes 52
  22.7 2.2 %copy-start.12 = (f32[576]{0:T(1024)S(1)}, f32[576]{0:T(1024)}, u32[]{:S(2)}) copy-start(f32[576]{0:T(1024)} %param.20) | copy-start | bytes 6916
  24.9 30.3 %copy-start.2 = (bf16[208,196]{1,0:T(8,128)(2,1)}, bf16[208,196]{1,0:T(8,128)(2,1)S(1)}, u32[]{:S(2)}) copy-start(bf16[208,196]{1,0:T(8,128)(2,1)S(1)} %reshape.486.pick_ref) | copy-start | bytes 244612
  35.9 7.3 %collective-permute-start = (bf16[4,28224]{1,0:T(4,128)(2,1)S(1)}, bf16[4,28224]{1,0:T(4,128)(2,1)S(1)}, u32[]{:S(2)}, u32[]{:S(2)}) collective-permute-start(bf16[4,28224]{1,0:T(4,128)(2,1)S(1)} %broadcast_select_fusion.2), channel_id=1, source_target_pairs={{0,1},{1,2},{2,3},{3,0},{4,5},{5,6},{6,7},{7,4},{8,9},{9,10},{10,1... | collective-permute-start | bytes 677384 | tf_op jit(solution)/shard_map/ppermute | solution.py:315
  36.0 8.4 %collective-permute-start.1 = (bf16[4,28224]{1,0:T(4,128)(2,1)S(1)}, bf16[4,28224]{1,0:T(4,128)(2,1)S(1)}, u32[]{:S(2)}, u32[]{:S(2)}) collective-permute-start(bf16[4,28224]{1,0:T(4,128)(2,1)S(1)} %broadcast_select_fusion.2), channel_id=1, source_target_pairs={{0,2},{1,3},{2,0},{3,1},{4,6},{5,7},{6,4},{7,5},{8,10},{9,11},{10,... | collective-permute-start | bytes 677384 | tf_op jit(solution)/shard_map/ppermute | solution.py:315
  36.6 10.1 %collective-permute-start.2 = (bf16[4,28224]{1,0:T(4,128)(2,1)S(1)}, bf16[4,28224]{1,0:T(4,128)(2,1)S(1)}, u32[]{:S(2)}, u32[]{:S(2)}) collective-permute-start(bf16[4,28224]{1,0:T(4,128)(2,1)S(1)} %broadcast_select_fusion.2), channel_id=1, source_target_pairs={{0,3},{1,0},{2,1},{3,2},{4,7},{5,4},{6,5},{7,6},{8,11},{9,8},{10,9... | collective-permute-start | bytes 677384 | tf_op jit(solution)/shard_map/ppermute | solution.py:315
  55.3 1.8 %copy-start.1 = (bf16[2,576,1152]{2,1,0:T(8,128)(2,1)S(1)}, bf16[2,576,1152]{2,1,0:T(8,128)(2,1)}, u32[]{:S(2)}) copy-start(bf16[2,576,1152]{2,1,0:T(8,128)(2,1)} %all_ref.1) | copy-start | bytes 7962628
  63.6 0.8 copy-start.3
  64.5 0.8 copy-start.4
  65.3 0.8 copy-start.5
  67.7 27.6 %all-to-all-start.1 = ((bf16[4,208,424]{2,0,1:T(4,128)(2,1)}), bf16[4,208,424]{2,0,1:T(4,128)(2,1)S(1)}, u32[]{:S(2)}, u32[]{:S(2)}) async-start(bf16[4,208,424]{2,0,1:T(4,128)(2,1)} %copy.93), calls=%async_computation.1 | async-start | bytes 1703936 | tf_op jit(solution)/shard_map/all_to_all | solution.py:360
  95.3 31.4 %all-to-all-start.2 = ((bf16[4,208,576]{2,0,1:T(4,128)(2,1)}), bf16[4,208,576]{2,0,1:T(4,128)(2,1)S(1)}, u32[]{:S(2)}, u32[]{:S(2)}) async-start(bf16[4,208,576]{2,0,1:T(4,128)(2,1)} %copy.103), calls=%async_computation.2 | async-start | bytes 2129920 | tf_op jit(solution)/shard_map/all_to_all | solution.py:360
  140.6 7.8 %collective-permute-start.6 = (bf16[4,49,576]{2,0,1:T(4,128)(2,1)S(1)}, bf16[4,49,576]{2,0,1:T(4,128)(2,1)S(1)}, u32[]{:S(2)}, u32[]{:S(2)}) collective-permute-start(bf16[4,49,576]{2,0,1:T(4,128)(2,1)S(1)} %get-tuple-element.21), channel_id=1, source_target_pairs={{0,1},{1,2},{2,3},{3,0},{4,5},{5,6},{6,7},{7,4},{8,9},{9,10},{10,1... | collective-permute-start | bytes 677384 | tf_op jit(solution)/shard_map/ppermute | solution.py:315
  140.7 8.9 %collective-permute-start.7 = (bf16[4,49,576]{2,0,1:T(4,128)(2,1)S(1)}, bf16[4,49,576]{2,0,1:T(4,128)(2,1)S(1)}, u32[]{:S(2)}, u32[]{:S(2)}) collective-permute-start(bf16[4,49,576]{2,0,1:T(4,128)(2,1)S(1)} %get-tuple-element.23), channel_id=1, source_target_pairs={{0,2},{1,3},{2,0},{3,1},{4,6},{5,7},{6,4},{7,5},{8,10},{9,11},{10,... | collective-permute-start | bytes 677384 | tf_op jit(solution)/shard_map/ppermute | solution.py:315
  141.3 11.2 %collective-permute-start.8 = (bf16[4,49,576]{2,0,1:T(4,128)(2,1)S(1)}, bf16[4,49,576]{2,0,1:T(4,128)(2,1)S(1)}, u32[]{:S(2)}, u32[]{:S(2)}) collective-permute-start(bf16[4,49,576]{2,0,1:T(4,128)(2,1)S(1)} %get-tuple-element.22), channel_id=1, source_target_pairs={{0,3},{1,0},{2,1},{3,2},{4,7},{5,4},{6,5},{7,6},{8,11},{9,8},{10,9... | collective-permute-start | bytes 677384 | tf_op jit(solution)/shard_map/ppermute | solution.py:315

commit v3 on v2

--- a/solution.py
+++ b/solution.py
@@ -76,10 +76,13 @@
         flat[k, pl.ds(start // 128 + t, rows, stride=STATE), :] = block[:, 128 * t : 128 * t + 128]
 
 
-def load_tiles(ref, k, start, size):
-    rows = ref.shape[1]
-    flat = ref.reshape(2, rows * STATE, 128)
-    parts = [flat[k, pl.ds(start // 128 + t, rows, stride=STATE), :] for t in range(size // 128)]
+def load_sums(ref, start, size):
+    rows, each = ref.shape[1], ref.shape[2]
+    flat = ref.reshape(2, rows * each, 128)
+    parts = []
+    for t in range(start // 128, (start + size) // 128):
+        terms = [flat[k, pl.ds(8 * t + s, rows, stride=each), :] for k in range(2) for s in range(8)]
+        parts.append(sum(terms[1:], terms[0]))
     return jnp.concatenate(parts, axis=1)
 
 
@@ -122,7 +125,8 @@
             d_now = jnp.broadcast_to(d_ref[k, row, t : t + 1, :], (STATE, 128))
             x_now = jnp.broadcast_to(x_ref[k, row, t : t + 1, :], (STATE, 128))
             h = jnp.exp2(d_now * rate_ref[k, :, cols]) * state[t] + x_now * b_now
-            y_ref[k, row, t : t + 1, :] = jnp.sum(h * c_now, axis=0, keepdims=True)
+            product = h * c_now
+            y_ref[k, row, 8 * t : 8 * t + 8, :] = product[0:8] + product[8:16]
             after.append(h)
         return tuple(after)
 
@@ -171,7 +175,7 @@
     pick = pick_ref[...]
     for start, size in chunks_of(part):
         cols = slice(start, start + size)
-        total = load_tiles(y_ref, 0, start, size) + load_tiles(y_ref, 1, start, size)
+        total = load_sums(y_ref, start, size)
         total = total + skip_ref[:, cols] * u_ref[:, cols]
         total = dot(pick, total.astype(BF16)).astype(BF16)
         if size == 512:
@@ -213,7 +217,7 @@
     scan(1, steps, 4, lambda i: row_at(i, True), scratch, rate_ref, y_ref)
     for start, size in chunks_of(part):
         cols = slice(start, start + size)
-        total = load_tiles(y_ref, 0, start, size) + load_tiles(y_ref, 1, start, size)
+        total = load_sums(y_ref, start, size)
         out_ref[:, cols] = total + skip_ref[:, cols] * u_ref[:, cols]
 
 
@@ -246,19 +250,30 @@
 
 
 def scan_scratch(rows, part):
-    return [pltpu.VMEM((rows, lanes_of(part)), F32)] + [pltpu.VMEM((2, rows, STATE, 128), F32)] * 5
+    lanes = lanes_of(part)
+    inputs = [pltpu.VMEM((2, rows, STATE, 128), F32)] * 4
+    return [pltpu.VMEM((rows, lanes), F32)] + inputs + [pltpu.VMEM((2, rows, lanes // 16, 128), F32)]
 
 
 def call(kernel, out_shape, scratch, flops, *operands):
+    specs, arrays = [], []
+    for operand in operands:
+        array, half = operand if isinstance(operand, tuple) else (operand, None)
+        arrays.append(array)
+        if half is None:
+            specs.append(pl.BlockSpec(memory_space=pltpu.VMEM))
+        else:
+            specs.append(pl.BlockSpec((2,) + array.shape[1:], functools.partial(lambda h, i: (h, 0, 0), half)))
     return pl.pallas_call(
         kernel,
+        grid=(1,),
         out_shape=out_shape,
-        in_specs=[pl.BlockSpec(memory_space=pltpu.VMEM)] * len(operands),
+        in_specs=specs,
         out_specs=pl.BlockSpec(memory_space=pltpu.VMEM),
         scratch_shapes=scratch,
         compiler_params=pltpu.CompilerParams(vmem_limit_bytes=56 * 1024 * 1024),
         cost_estimate=pl.CostEstimate(flops=flops, bytes_accessed=8_000_000, transcendentals=7_000_000),
-    )(*operands)
+    )(*arrays)
 
 
 def body(
@@ -323,7 +338,7 @@
     sender = jnp.sum((offsets[None, :] <= wanted[:, None]).astype(jnp.int32), axis=1) - 1
     lane_of = (wanted - offsets[sender]) // owners
     owned = jnp.take(arrived, sender * capacity + lane_of, axis=0)
-    full = jnp.swapaxes(gathered(owned), 0, 1).reshape(OWN_BLK, patches, width)
+    full = lax.all_gather(owned, "space", axis=1, tiled=True).reshape(OWN_BLK, patches, width)
 
     def per_frame(*dims):
         return pl.BlockSpec((1,) + dims, lambda i: (i, 0, 0))
@@ -367,7 +382,7 @@
         jax.ShapeDtypeStruct((OWN_BLK, owners * slots, 2 * part), BF16),
         scan_scratch(patches, part),
         20_000_000_000,
-        inner, stats, gate, pick, perm, inverse, spread, dt_wide[:2], bias[:2], rate[:2],
+        inner, stats, gate, pick, perm, inverse, spread, (dt_wide, 0), (bias, 0), (rate, 0),
         (skip[0] + skip[1])[None, :],
     )
     late = to_owner(late)
@@ -386,7 +401,7 @@
         jax.ShapeDtypeStruct((rows, lanes_of(part)), F32),
         scan_scratch(rows, part),
         20_000_000_000,
-        early, closed, perm, spread, dt_wide[2:], bias[2:], rate[2:], (skip[2] + skip[3])[None, :],
+        early, closed, perm, spread, (dt_wide, 1), (bias, 1), (rate, 1), (skip[2] + skip[3])[None, :],
     )
     term = call(
         output_kernel,
@@ -398,11 +413,8 @@
     term = term.reshape(ROWS, owners, OWN_BLK, groups, width)
     term = jnp.transpose(term, (2, 1, 0, 3, 4)).reshape(frames_total, slots, width)[:, :per_owner]
     term = term.reshape(spaces, frames_total // spaces, per_owner, width)
-    mixed = 0.0
-    for k in range(spaces):
-        piece = lax.dynamic_index_in_dim(term, (space_index + k) % spaces, 0, keepdims=False)
-        mixed = mixed + (to_next(piece, k) if k else piece).astype(F32)
-    mixed = mixed.astype(BF16)
+    term = lax.all_to_all(term, "space", split_axis=0, concat_axis=0, tiled=True)
+    mixed = jnp.sum(term.astype(F32), axis=0).astype(BF16)
     return jnp.swapaxes(mixed, 0, 1).reshape(per_owner, frames_total // spaces * width)
 
 

time: 156 us -> 146 us (0.936)
  blocking collectives: 0 us -> 25 us
  waiting for transfers between devices: 24 us -> 6.74 us
  local copies, waits for them, and re-layouts: 42.5 us -> 34.3 us
  starting transfers between devices: 22.5 us -> 18.2 us
  Pallas kernels: 51.1 us -> 47.7 us
  other arithmetic: 9.91 us -> 8.29 us
    ppermute x9 -> x3, waiting for transfers between devices: 18.4 us -> 0.01 us  [to_next(): lax.ppermute(array, 'space', [(i, (i + k) % spaces) for i in range(spaces)])]
    all_to_all x0 -> x1, blocking collectives: none -> 16.5 us  [body(): lax.all_to_all(term, 'space', split_axis=0, concat_axis=0, tiled=True)]
    all_gather x0 -> x1, blocking collectives: none -> 8.46 us  [body(): lax.all_gather(owned, 'space', axis=1, tiled=True)]
    slice x7 -> x0, local copies, waits for them, and re-layouts: 4.7 us -> none  [the longest x2 1.84 us: body(): dt_wide[:2]]
    ppermute x9 -> x3, starting transfers between devices: 8.58 us -> 4.46 us  [to_next(): lax.ppermute(array, 'space', [(i, (i + k) % spaces) for i in range(spaces)])]
    pallas_call x3, Pallas kernels: 44.6 us -> 41.1 us  [call(): pl.pallas_call(kernel, grid=(1,), out_shape=out_shape, in_specs=specs, ou...]
    gather x3 -> x2, local copies, waits for them, and re-layouts: 4.27 us -> 2.08 us  [gathered(): return jnp.take(jnp.stack(shares), order, axis=0)]
    another operation x2 -> x1, other arithmetic: 2.06 us -> 0.21 us  [gathered(): return jnp.take(jnp.stack(shares), order, axis=0)]
  transfers between devices with their start and end apart: 12 -> 6, of which waited for: 8 -> 2; matrix products, arithmetic and copies ran while one was open for 15% -> 15% of each run, Pallas kernels for 25% -> 24%
where the time goes in v3:
time: 146 us; the launch traced here: 145 us
  Pallas kernels  47.7 us (33%)
  local copies, waits for them, and re-layouts  34.3 us (23%)
  blocking collectives  25 us (17%)
  starting transfers between devices  18.2 us (12%)
  other arithmetic  8.29 us (6%)
  waiting for transfers between devices  6.74 us (5%)
  matrix products  4.3 us (3%)
    pallas_call x3, Pallas kernels, call(): pl.pallas_call(kernel, grid=(1,), out_shape=out_shape, in_specs=specs, ou...  41.1 us
    all_to_all x1, blocking collectives, body(): lax.all_to_all(term, 'space', split_axis=0, concat_axis=0, tiled=True)  16.5 us
    all_to_all x2, starting transfers between devices, to_owner(): moved = lax.all_to_all(array, 'tm', split_axis=1, concat_axis=0, tiled=True)  8.84 us
    all_gather x1, blocking collectives, body(): lax.all_gather(owned, 'space', axis=1, tiled=True)  8.46 us
    all_to_all x2, waiting for transfers between devices, to_owner(): moved = lax.all_to_all(array, 'tm', split_axis=1, concat_axis=0, tiled=True)  6.73 us
    pallas_call x1, Pallas kernels, body(): pl.pallas_call(first_kernel, grid=(OWN_BLK,), out_shape=(jax.ShapeDtypeSt...  6.58 us
    unnamed x31, local copies, waits for them, and re-layouts  6.01 us
    all_to_all x1, starting transfers between devices, body(): lax.all_to_all(packed, 'tm', split_axis=0, concat_axis=0, tiled=True)  4.87 us
  transfers between devices with their start and end apart: 6, of which 2 were waited for; matrix products, arithmetic and copies ran while one was open for 15% of the time, Pallas kernels for 24%

profile of v3, /device:TPU:0, one launch (start us, length us, event | category | flops | bytes accessed | tf_op | source)
XLA Modules:
  0.0 145.0 jit_solution(1695576171922618354)
XLA Ops:
  0.0 0.9 reduce-window.16
  0.9 0.7 bitcast_subtract_fusion.2
  1.5 0.6 dynamic_slice.6
  2.1 0.7 and_select_fusion.7
  3.1 0.8 gather_fusion.1
  4.2 0.5 concatenate.3
  4.6 0.5 collective-permute-start
  5.1 2.6 %collective-permute-start.1 = (bf16[288,272]{0,1:T(8,128)(2,1)S(1)}, bf16[288,272]{0,1:T(8,128)(2,1)S(1)}, u32[]{:S(2)}, u32[]{:S(2)}) collective-permute-start(bf16[288,272]{0,1:T(8,128)(2,1)S(1)} %concatenate.3), channel_id=1, source_target_pairs={{0,2},{1,3},{2,0},{3,1},{4,6},{5,7},{6,4},{7,5},{8,10},{9,11},{10,... | collective-permute-start | bytes 470024 | tf_op jit(solution)/shard_map/ppermute | solution.py:330
  7.7 1.4 collective-permute-start.2
  9.1 1.0 all_to_all.33
  10.1 4.9 %all-to-all-start = ((bf16[4,2,28224]{2,1,0:T(2,128)(2,1)}), bf16[4,2,28224]{2,1,0:T(2,128)(2,1)}, u32[]{:S(2)}, u32[]{:S(2)}) async-start(bf16[4,2,28224]{2,1,0:T(2,128)(2,1)} %all_to_all.33), calls=%async_computation | async-start | bytes 905216 | tf_op jit(solution)/shard_map/all_to_all | solution.py:320
  14.9 0.2 convert_reduce_fusion
  15.1 0.6 gather_fusion
  15.9 1.6 %fusion = bf16[4,36,1152]{2,1,0:T(8,128)(2,1)S(1)} fusion(bf16[288,1152,1]{1,0,2:T(8,128)(2,1)} %constant.179, bf16[4,36,288]{2,0,1:T(4,128)(2,1)S(1)} %copy-done.14), kind=kOutput, calls=%fused_computation.5 | convolution fusion | flops 95717376 | bytes 1078272 | tf_op jit(solution)/shard_map/kic,cn->kin/dot_general | solution.py:302
  17.9 1.1 fusion.20
  19.0 0.7 multiply_bitcast_fusion.rate_ref
  19.8 0.8 convolution_bitcast_fusion.1
  20.6 0.8 convolution_bitcast_fusion
  21.4 0.6 slice_add_fusion
  22.2 1.6 %constant_dynamic-slice_fusion.w_ref = bf16[2,576,288]{2,1,0:T(8,128)(2,1)S(1)} fusion(bf16[2,576,1152]{2,1,0:T(8,128)(2,1)} %all_ref.1, s32[]{:T(128)S(6)} %select_n.206), kind=kLoop, calls=%fused_computation.108 | loop fusion | bytes 1327108 | tf_op jit(solution)/shard_map/dynamic_slice | solution.py:294
  23.8 0.3 broadcast_in_dim.97
  24.2 1.4 copy_select_fusion.dt_ref
  26.2 0.6 broadcast_in_dim.100.bias_ref
  27.0 0.8 copy.95.closed_ref
  27.8 0.2 pad_maximum_fusion
  28.0 0.7 gather_fusion.3
  28.7 1.3 copy.86
  30.1 1.4 bitcast_select_fusion.proj_ref
  31.5 1.3 all_to_all.35
  32.8 0.8 gather_fusion.2
  33.7 8.5 %all-gather = bf16[4,28224,4]{1,2,0:T(4,128)(2,1)S(1)} all-gather(bf16[1,28224,4]{1,2,0:T(4,128)(2,1)S(1)} %select_bitcast_fusion), channel_id=1, replica_groups=mesh['groups'=2,'tm'=4,'space'=4] {'space'}, dimensions={0}, use_global_device_ids=true | all-gather | bytes 1128960 | tf_op jit(solution)/shard_map/all_gather | solution.py:341
  42.2 0.3 copy.77
  42.5 1.8 %reshape.504 = bf16[112896,4]{0,1:T(4,128)(2,1)} reshape(bf16[4,28224,4]{1,0,2:T(4,128)(2,1)S(1)} %copy.77) | data formatting | bytes 1806336
  44.3 2.0 %reshape.457.x_ref = bf16[4,196,576]{2,1,0:T(8,128)(2,1)S(1)} reshape(bf16[4,112896]{1,0:T(4,128)(2,1)} %bitcast.114) | data formatting | bytes 1806336 | tf_op jit(solution)/shard_map/reshape | solution.py:341
  46.4 1.7 %copy-done.1 = bf16[2,576,1152]{2,1,0:T(8,128)(2,1)S(1)} copy-done((bf16[2,576,1152]{2,1,0:T(8,128)(2,1)S(1)}, bf16[2,576,1152]{2,1,0:T(8,128)(2,1)}, u32[]{:S(2)}) %copy-start.1) | copy-done | bytes 2654232
  48.1 6.6 %shard_map.154 = (bf16[4,196,288]{2,1,0:T(8,128)(2,1)S(1)}, bf16[4,196,136]{2,1,0:T(8,128)(2,1)S(1)}, bf16[4,208,424]{2,1,0:T(8,128)(2,1)S(1)}, bf16[4,208,288]{2,1,0:T(8,128)(2,1)S(1)}) custom-call(bf16[4,196,576]{2,1,0:T(8,128)(2,1)S(1)} %reshape.457.x_ref, bf16[2,576,288]{2,1,0:T(8,128)(2,1)S(1)} %constant_dynamic-slice_fusion.w_ref, ...), custom_call_target="tpu_custom_call" | custom-call | flops 4000000000 | bytes 4000000 | tf_op jit(solution)/shard_map/pallas_call | solution.py:350
  54.7 0.8 copy-done.3
  55.6 0.8 copy-done.4
  56.4 0.7 copy-done.5
  57.1 1.6 %copy.88 = bf16[4,208,424]{2,0,1:T(4,128)(2,1)} copy(bf16[4,208,424]{2,1,0:T(8,128)(2,1)S(1)} %get-tuple-element.13) | data formatting | bytes 1411072 | tf_op jit(solution)/shard_map/pallas_call | solution.py:350
  58.7 5.1 %all-to-all-start.1 = ((bf16[4,208,424]{2,0,1:T(4,128)(2,1)}), bf16[4,208,424]{2,0,1:T(4,128)(2,1)S(1)}, u32[]{:S(2)}, u32[]{:S(2)}) async-start(bf16[4,208,424]{2,0,1:T(4,128)(2,1)} %copy.88), calls=%async_computation.1 | async-start | bytes 1703936 | tf_op jit(solution)/shard_map/all_to_all | solution.py:375
  63.8 17.1 %shard_map.156 = bf16[4,208,576]{2,1,0:T(8,128)(2,1)} custom-call(bf16[4,196,288]{2,1,0:T(8,128)(2,1)} %copy-done.4, bf16[4,196,136]{2,1,0:T(8,128)(2,1)} %copy-done.5, bf16[4,208,288]{2,1,0:T(8,128)(2,1)} %copy-done.3, bf16[208,196]{1,0:T(8,128)(2,1)} %copy-done.2, bf16[512,512]{1,0:T(8,128)(2,1)} %constant.174.clone.perm_ref.inverse_ref, ...), custom_call_target="tpu_custom_call" | custom-call | flops 20000000000 | bytes 8000000 | tf_op jit(solution)/shard_map/pallas_call | solution.py:267
  80.9 2.6 %copy.96 = bf16[4,208,576]{2,0,1:T(4,128)(2,1)} copy(bf16[4,208,576]{2,1,0:T(8,128)(2,1)} %shard_map.156) | data formatting | bytes 1916928 | tf_op jit(solution)/shard_map/pallas_call | solution.py:267
  83.5 2.3 %all-to-all-done.1 = bf16[4,208,424]{2,0,1:T(4,128)(2,1)S(1)} async-done(((bf16[4,208,424]{2,0,1:T(4,128)(2,1)}), bf16[4,208,424]{2,0,1:T(4,128)(2,1)S(1)}, u32[]{:S(2)}, u32[]{:S(2)}) %all-to-all-start.1) | async-done | bytes 705568 | tf_op jit(solution)/shard_map/all_to_all | solution.py:375
  85.8 3.7 %all-to-all-start.2 = ((bf16[4,208,576]{2,0,1:T(4,128)(2,1)}), bf16[4,208,576]{2,0,1:T(4,128)(2,1)S(1)}, u32[]{:S(2)}, u32[]{:S(2)}) async-start(bf16[4,208,576]{2,0,1:T(4,128)(2,1)} %copy.96), calls=%async_computation.2 | async-start | bytes 2129920 | tf_op jit(solution)/shard_map/all_to_all | solution.py:375
  89.6 0.5 copy.89
  90.0 0.5 reshape.460
  90.5 0.7 copy.90
  91.2 1.1 copy.94.moved_ref
  92.2 18.4 %shard_map.155.temporal_ref = f32[208,1152]{1,0:T(8,128)} custom-call(bf16[4,208,424]{2,1,0:T(8,128)(2,1)} %copy.94.moved_ref, f32[208,2]{1,0:T(8,128)} %copy.95.closed_ref, bf16[512,512]{1,0:T(8,128)(2,1)} %constant.174.clone.perm_ref.inverse_ref, bf16[64,2048]{1,0:T(8,128)(2,1)} %constant.175.clone.spread_ref, ...), custom_call_target="tpu_custom_call" | custom-call | flops 20000000000 | bytes 8000000 | tf_op jit(solution)/shard_map/pallas_call | solution.py:267
  110.7 4.4 %all-to-all-done.2 = bf16[4,208,576]{2,0,1:T(4,128)(2,1)S(1)} async-done(((bf16[4,208,576]{2,0,1:T(4,128)(2,1)}), bf16[4,208,576]{2,0,1:T(4,128)(2,1)S(1)}, u32[]{:S(2)}, u32[]{:S(2)}) %all-to-all-start.2) | async-done | bytes 958496 | tf_op jit(solution)/shard_map/all_to_all | solution.py:375
  115.1 0.4 copy.97
  115.4 0.8 reshape.465
  116.3 0.4 copy.98
  116.7 1.1 copy.99.moved_ref
  117.8 5.6 %shard_map.157 = bf16[4,208,576]{2,1,0:T(8,128)(2,1)} custom-call(f32[208,1152]{1,0:T(8,128)} %shard_map.155.temporal_ref, bf16[4,208,576]{2,1,0:T(8,128)(2,1)} %copy.99.moved_ref, bf16[512,512]{1,0:T(8,128)(2,1)} %constant.174.clone.perm_ref.inverse_ref, bf16[512,512]{1,0:T(8,128)(2,1)} %constant.174.clone.perm_ref.inverse_ref, bf16[288,576]{1,0:T(8,128)(2,1)} %w_ref.1), custom_call_target="tpu_custom_call" | custom-call | flops 2000000000 | bytes 8000000 | tf_op jit(solution)/shard_map/pallas_call | solution.py:267
  123.4 1.6 %copy.100 = bf16[4,208,576]{2,0,1:T(4,128)(2,1)S(1)} copy(bf16[4,208,576]{2,1,0:T(8,128)(2,1)} %shard_map.157) | data formatting | bytes 1916928 | tf_op jit(solution)/shard_map/pallas_call | solution.py:267
  125.0 0.4 copy.101
  125.5 0.6 reshape.468
  126.1 0.3 reshape.469
  126.4 0.3 copy.102
  126.7 16.5 %all_to_all.47 = bf16[4,4,49,576]{3,1,2,0:T(4,128)(2,1)S(1)} all-to-all(bf16[4,4,49,576]{3,1,2,0:T(4,128)(2,1)S(1)} %copy.102), channel_id=1, replica_groups=mesh['groups'=2,'tm'=4,'space'=4] {'space'}, dimensions={0} | all-to-all | bytes 1806336 | tf_op jit(solution)/shard_map/all_to_all | solution.py:416
  143.3 0.7 reduce_sum.22
  144.0 1.0 reshape.470
  (72 shorter events, 2.0 us)
Async XLA Ops:
  0.0 3.1 %copy-start = (bf16[8,28224]{1,0:T(8,128)(2,1)S(1)}, bf16[8,28224]{1,0:T(8,128)(2,1)}, u32[]{:S(2)}) copy-start(bf16[8,28224]{1,0:T(8,128)(2,1)} %param.16) | copy-start | bytes 1354756
  3.1 1.0 copy-start.7
  4.2 11.7 %copy-start.8 = (s32[196,196]{1,0:T(8,128)S(1)}, s32[196,196]{1,0:T(8,128)}, u32[]{:S(2)}) copy-start(s32[196,196]{1,0:T(8,128)} %param.19) | copy-start | bytes 460996
  4.6 11.3 %copy-start.14 = (bf16[4,36,288]{2,0,1:T(4,128)(2,1)S(1)}, bf16[4,36,288]{2,0,1:T(4,128)(2,1)}, u32[]{:S(2)}) copy-start(bf16[4,36,288]{2,0,1:T(4,128)(2,1)} %param.23) | copy-start | bytes 248836
  4.6 23.1 %collective-permute-start = (bf16[288,272]{0,1:T(8,128)(2,1)S(1)}, bf16[288,272]{0,1:T(8,128)(2,1)S(1)}, u32[]{:S(2)}, u32[]{:S(2)}) collective-permute-start(bf16[288,272]{0,1:T(8,128)(2,1)S(1)} %concatenate.3), channel_id=1, source_target_pairs={{0,1},{1,2},{2,3},{3,0},{4,5},{5,6},{6,7},{7,4},{8,9},{9,10},{10,1... | collective-permute-start | bytes 470024 | tf_op jit(solution)/shard_map/ppermute | solution.py:330
  5.1 22.6 %collective-permute-start.1 = (bf16[288,272]{0,1:T(8,128)(2,1)S(1)}, bf16[288,272]{0,1:T(8,128)(2,1)S(1)}, u32[]{:S(2)}, u32[]{:S(2)}) collective-permute-start(bf16[288,272]{0,1:T(8,128)(2,1)S(1)} %concatenate.3), channel_id=1, source_target_pairs={{0,2},{1,3},{2,0},{3,1},{4,6},{5,7},{6,4},{7,5},{8,10},{9,11},{10,... | collective-permute-start | bytes 470024 | tf_op jit(solution)/shard_map/ppermute | solution.py:330
  7.7 20.0 %collective-permute-start.2 = (bf16[288,272]{0,1:T(8,128)(2,1)S(1)}, bf16[288,272]{0,1:T(8,128)(2,1)S(1)}, u32[]{:S(2)}, u32[]{:S(2)}) collective-permute-start(bf16[288,272]{0,1:T(8,128)(2,1)S(1)} %concatenate.3), channel_id=1, source_target_pairs={{0,3},{1,0},{2,1},{3,2},{4,7},{5,4},{6,5},{7,6},{8,11},{9,8},{10,9... | collective-permute-start | bytes 470024 | tf_op jit(solution)/shard_map/ppermute | solution.py:330
  10.1 21.4 %all-to-all-start = ((bf16[4,2,28224]{2,1,0:T(2,128)(2,1)}), bf16[4,2,28224]{2,1,0:T(2,128)(2,1)}, u32[]{:S(2)}, u32[]{:S(2)}) async-start(bf16[4,2,28224]{2,1,0:T(2,128)(2,1)} %all_to_all.33), calls=%async_computation | async-start | bytes 905216 | tf_op jit(solution)/shard_map/all_to_all | solution.py:320
  15.9 1.9 %copy-start.6 = (f32[288,1152]{1,0:T(8,128)S(1)}, f32[288,1152]{1,0:T(8,128)}, u32[]{:S(2)}) copy-start(f32[288,1152]{1,0:T(8,128)} %constant.173.clone) | copy-start | bytes 3981316
  15.9 1.9 %copy-start.9 = (f32[4,288,16]{1,2,0:T(8,128)S(1)}, f32[4,288,16]{1,2,0:T(8,128)}, u32[]{:S(2)}) copy-start(f32[4,288,16]{1,2,0:T(8,128)} %param.25) | copy-start | bytes 221188
  17.7 2.0 %copy-start.10 = (f32[4,288]{1,0:T(4,128)S(1)}, f32[4,288]{1,0:T(4,128)}, u32[]{:S(2)}) copy-start(f32[4,288]{1,0:T(4,128)} %param.24) | copy-start | bytes 13828
  19.0 1.6 %copy-start.11 = (f32[4,288]{1,0:T(4,128)S(1)}, f32[4,288]{1,0:T(4,128)}, u32[]{:S(2)}) copy-start(f32[4,288]{1,0:T(4,128)} %param.26) | copy-start | bytes 13828
  19.8 2.2 %copy-start.13 = (s32[4]{0:T(128)S(1)}, s32[4]{0:T(128)}, u32[]{:S(2)}) copy-start(s32[4]{0:T(128)} %param.18) | copy-start | bytes 52
  24.2 2.0 %copy-start.12 = (f32[576]{0:T(1024)S(1)}, f32[576]{0:T(1024)}, u32[]{:S(2)}) copy-start(f32[576]{0:T(1024)} %param.20) | copy-start | bytes 6916
  26.1 20.2 %copy-start.2 = (bf16[208,196]{1,0:T(8,128)(2,1)}, bf16[208,196]{1,0:T(8,128)(2,1)S(1)}, u32[]{:S(2)}) copy-start(bf16[208,196]{1,0:T(8,128)(2,1)S(1)} %reshape.459.pick_ref) | copy-start | bytes 244612
  46.4 1.8 %copy-start.1 = (bf16[2,576,1152]{2,1,0:T(8,128)(2,1)S(1)}, bf16[2,576,1152]{2,1,0:T(8,128)(2,1)}, u32[]{:S(2)}) copy-start(bf16[2,576,1152]{2,1,0:T(8,128)(2,1)} %all_ref.1) | copy-start | bytes 7962628
  54.7 0.8 copy-start.3
  55.6 0.8 copy-start.4
  56.4 0.8 copy-start.5
  58.7 27.1 %all-to-all-start.1 = ((bf16[4,208,424]{2,0,1:T(4,128)(2,1)}), bf16[4,208,424]{2,0,1:T(4,128)(2,1)S(1)}, u32[]{:S(2)}, u32[]{:S(2)}) async-start(bf16[4,208,424]{2,0,1:T(4,128)(2,1)} %copy.88), calls=%async_computation.1 | async-start | bytes 1703936 | tf_op jit(solution)/shard_map/all_to_all | solution.py:375
  85.8 29.2 %all-to-all-start.2 = ((bf16[4,208,576]{2,0,1:T(4,128)(2,1)}), bf16[4,208,576]{2,0,1:T(4,128)(2,1)S(1)}, u32[]{:S(2)}, u32[]{:S(2)}) async-start(bf16[4,208,576]{2,0,1:T(4,128)(2,1)} %copy.96), calls=%async_computation.2 | async-start | bytes 2129920 | tf_op jit(solution)/shard_map/all_to_all | solution.py:375

commit v4 on v3

--- a/solution.py
+++ b/solution.py
@@ -170,8 +170,8 @@
         lambda r: inner_ref[r, :, cut:],
     )
     prepare(part, values, stats_ref, 0, None, (perm_ref, spread_ref, dt_ref, bias_ref), scratch)
-    scan(0, length, 4, lambda i: i, scratch, rate_ref, y_ref)
-    scan(1, length, 4, lambda i: length - 1 - i, scratch, rate_ref, y_ref)
+    scan(0, length, 7, lambda i: i, scratch, rate_ref, y_ref)
+    scan(1, length, 7, lambda i: length - 1 - i, scratch, rate_ref, y_ref)
     pick = pick_ref[...]
     for start, size in chunks_of(part):
         cols = slice(start, start + size)
@@ -213,8 +213,8 @@
         return ((frame % owners) * OWN_BLK + frame // owners) * groups + group
 
     steps = frames * groups
-    scan(0, steps, 4, lambda i: row_at(i, False), scratch, rate_ref, y_ref)
-    scan(1, steps, 4, lambda i: row_at(i, True), scratch, rate_ref, y_ref)
+    scan(0, steps, 8, lambda i: row_at(i, False), scratch, rate_ref, y_ref)
+    scan(1, steps, 8, lambda i: row_at(i, True), scratch, rate_ref, y_ref)
     for start, size in chunks_of(part):
         cols = slice(start, start + size)
         total = load_sums(y_ref, start, size)

time: 146 us -> 146 us (level)
  no operation moved by 1% of the time
where the time goes in v4:
time: 146 us; the launch traced here: 145 us
  Pallas kernels  47.7 us (33%)
  local copies, waits for them, and re-layouts  34.3 us (23%)
  blocking collectives  25 us (17%)
  starting transfers between devices  18.2 us (12%)
  other arithmetic  8.29 us (6%)
  waiting for transfers between devices  6.91 us (5%)
  matrix products  4.3 us (3%)
    pallas_call x3, Pallas kernels, call(): pl.pallas_call(kernel, grid=(1,), out_shape=out_shape, in_specs=specs, ou...  41.1 us
    all_to_all x1, blocking collectives, body(): lax.all_to_all(term, 'space', split_axis=0, concat_axis=0, tiled=True)  16.5 us
    all_to_all x2, starting transfers between devices, to_owner(): moved = lax.all_to_all(array, 'tm', split_axis=1, concat_axis=0, tiled=True)  8.84 us
    all_gather x1, blocking collectives, body(): lax.all_gather(owned, 'space', axis=1, tiled=True)  8.46 us
    all_to_all x2, waiting for transfers between devices, to_owner(): moved = lax.all_to_all(array, 'tm', split_axis=1, concat_axis=0, tiled=True)  6.9 us
    pallas_call x1, Pallas kernels, body(): pl.pallas_call(first_kernel, grid=(OWN_BLK,), out_shape=(jax.ShapeDtypeSt...  6.58 us
    unnamed x31, local copies, waits for them, and re-layouts  6.01 us
    all_to_all x1, starting transfers between devices, body(): lax.all_to_all(packed, 'tm', split_axis=0, concat_axis=0, tiled=True)  4.87 us
  transfers between devices with their start and end apart: 6, of which 2 were waited for; matrix products, arithmetic and copies ran while one was open for 15% of the time, Pallas kernels for 24%

profile of v4, /device:TPU:0, one launch (start us, length us, event | category | flops | bytes accessed | tf_op | source)
XLA Modules:
  0.0 145.3 jit_solution(11895990126835781860)
XLA Ops:
  0.0 0.9 reduce-window.16
  0.9 0.7 bitcast_subtract_fusion.2
  1.5 0.6 dynamic_slice.6
  2.1 0.7 and_select_fusion.7
  3.1 0.8 gather_fusion.1
  4.2 0.5 concatenate.3
  4.6 0.5 collective-permute-start
  5.1 2.6 %collective-permute-start.1 = (bf16[288,272]{0,1:T(8,128)(2,1)S(1)}, bf16[288,272]{0,1:T(8,128)(2,1)S(1)}, u32[]{:S(2)}, u32[]{:S(2)}) collective-permute-start(bf16[288,272]{0,1:T(8,128)(2,1)S(1)} %concatenate.3), channel_id=1, source_target_pairs={{0,2},{1,3},{2,0},{3,1},{4,6},{5,7},{6,4},{7,5},{8,10},{9,11},{10,... | collective-permute-start | bytes 470024 | tf_op jit(solution)/shard_map/ppermute | solution.py:330
  7.7 1.4 collective-permute-start.2
  9.1 1.0 all_to_all.33
  10.1 4.9 %all-to-all-start = ((bf16[4,2,28224]{2,1,0:T(2,128)(2,1)}), bf16[4,2,28224]{2,1,0:T(2,128)(2,1)}, u32[]{:S(2)}, u32[]{:S(2)}) async-start(bf16[4,2,28224]{2,1,0:T(2,128)(2,1)} %all_to_all.33), calls=%async_computation | async-start | bytes 905216 | tf_op jit(solution)/shard_map/all_to_all | solution.py:320
  14.9 0.2 convert_reduce_fusion
  15.1 0.6 gather_fusion
  15.9 1.6 %fusion = bf16[4,36,1152]{2,1,0:T(8,128)(2,1)S(1)} fusion(bf16[288,1152,1]{1,0,2:T(8,128)(2,1)} %constant.179, bf16[4,36,288]{2,0,1:T(4,128)(2,1)S(1)} %copy-done.14), kind=kOutput, calls=%fused_computation.5 | convolution fusion | flops 95717376 | bytes 1078272 | tf_op jit(solution)/shard_map/kic,cn->kin/dot_general | solution.py:302
  17.9 1.1 fusion.20
  19.0 0.7 multiply_bitcast_fusion.rate_ref
  19.8 0.8 convolution_bitcast_fusion.1
  20.6 0.8 convolution_bitcast_fusion
  21.4 0.6 slice_add_fusion
  22.2 1.6 %constant_dynamic-slice_fusion.w_ref = bf16[2,576,288]{2,1,0:T(8,128)(2,1)S(1)} fusion(bf16[2,576,1152]{2,1,0:T(8,128)(2,1)} %all_ref.1, s32[]{:T(128)S(6)} %select_n.206), kind=kLoop, calls=%fused_computation.108 | loop fusion | bytes 1327108 | tf_op jit(solution)/shard_map/dynamic_slice | solution.py:294
  23.8 0.3 broadcast_in_dim.97
  24.2 1.4 copy_select_fusion.dt_ref
  26.2 0.6 broadcast_in_dim.100.bias_ref
  27.0 0.8 copy.95.closed_ref
  27.8 0.2 pad_maximum_fusion
  28.0 0.7 gather_fusion.3
  28.7 1.3 copy.86
  30.1 1.4 bitcast_select_fusion.proj_ref
  31.5 1.3 all_to_all.35
  32.8 0.8 gather_fusion.2
  33.7 8.5 %all-gather = bf16[4,28224,4]{1,2,0:T(4,128)(2,1)S(1)} all-gather(bf16[1,28224,4]{1,2,0:T(4,128)(2,1)S(1)} %select_bitcast_fusion), channel_id=1, replica_groups=mesh['groups'=2,'tm'=4,'space'=4] {'space'}, dimensions={0}, use_global_device_ids=true | all-gather | bytes 1128960 | tf_op jit(solution)/shard_map/all_gather | solution.py:341
  42.2 0.3 copy.77
  42.5 1.8 %reshape.504 = bf16[112896,4]{0,1:T(4,128)(2,1)} reshape(bf16[4,28224,4]{1,0,2:T(4,128)(2,1)S(1)} %copy.77) | data formatting | bytes 1806336
  44.3 2.0 %reshape.457.x_ref = bf16[4,196,576]{2,1,0:T(8,128)(2,1)S(1)} reshape(bf16[4,112896]{1,0:T(4,128)(2,1)} %bitcast.114) | data formatting | bytes 1806336 | tf_op jit(solution)/shard_map/reshape | solution.py:341
  46.4 1.7 %copy-done.1 = bf16[2,576,1152]{2,1,0:T(8,128)(2,1)S(1)} copy-done((bf16[2,576,1152]{2,1,0:T(8,128)(2,1)S(1)}, bf16[2,576,1152]{2,1,0:T(8,128)(2,1)}, u32[]{:S(2)}) %copy-start.1) | copy-done | bytes 2654232
  48.1 6.6 %shard_map.154 = (bf16[4,196,288]{2,1,0:T(8,128)(2,1)S(1)}, bf16[4,196,136]{2,1,0:T(8,128)(2,1)S(1)}, bf16[4,208,424]{2,1,0:T(8,128)(2,1)S(1)}, bf16[4,208,288]{2,1,0:T(8,128)(2,1)S(1)}) custom-call(bf16[4,196,576]{2,1,0:T(8,128)(2,1)S(1)} %reshape.457.x_ref, bf16[2,576,288]{2,1,0:T(8,128)(2,1)S(1)} %constant_dynamic-slice_fusion.w_ref, ...), custom_call_target="tpu_custom_call" | custom-call | flops 4000000000 | bytes 4000000 | tf_op jit(solution)/shard_map/pallas_call | solution.py:350
  54.7 0.8 copy-done.3
  55.6 0.8 copy-done.4
  56.4 0.7 copy-done.5
  57.1 1.6 %copy.88 = bf16[4,208,424]{2,0,1:T(4,128)(2,1)} copy(bf16[4,208,424]{2,1,0:T(8,128)(2,1)S(1)} %get-tuple-element.13) | data formatting | bytes 1411072 | tf_op jit(solution)/shard_map/pallas_call | solution.py:350
  58.7 5.1 %all-to-all-start.1 = ((bf16[4,208,424]{2,0,1:T(4,128)(2,1)}), bf16[4,208,424]{2,0,1:T(4,128)(2,1)S(1)}, u32[]{:S(2)}, u32[]{:S(2)}) async-start(bf16[4,208,424]{2,0,1:T(4,128)(2,1)} %copy.88), calls=%async_computation.1 | async-start | bytes 1703936 | tf_op jit(solution)/shard_map/all_to_all | solution.py:375
  63.8 16.9 %shard_map.156 = bf16[4,208,576]{2,1,0:T(8,128)(2,1)} custom-call(bf16[4,196,288]{2,1,0:T(8,128)(2,1)} %copy-done.4, bf16[4,196,136]{2,1,0:T(8,128)(2,1)} %copy-done.5, bf16[4,208,288]{2,1,0:T(8,128)(2,1)} %copy-done.3, bf16[208,196]{1,0:T(8,128)(2,1)} %copy-done.2, bf16[512,512]{1,0:T(8,128)(2,1)} %constant.174.clone.perm_ref.inverse_ref, ...), custom_call_target="tpu_custom_call" | custom-call | flops 20000000000 | bytes 8000000 | tf_op jit(solution)/shard_map/pallas_call | solution.py:267
  80.7 2.6 %copy.96 = bf16[4,208,576]{2,0,1:T(4,128)(2,1)} copy(bf16[4,208,576]{2,1,0:T(8,128)(2,1)} %shard_map.156) | data formatting | bytes 1916928 | tf_op jit(solution)/shard_map/pallas_call | solution.py:267
  83.3 2.5 %all-to-all-done.1 = bf16[4,208,424]{2,0,1:T(4,128)(2,1)S(1)} async-done(((bf16[4,208,424]{2,0,1:T(4,128)(2,1)}), bf16[4,208,424]{2,0,1:T(4,128)(2,1)S(1)}, u32[]{:S(2)}, u32[]{:S(2)}) %all-to-all-start.1) | async-done | bytes 705568 | tf_op jit(solution)/shard_map/all_to_all | solution.py:375
  85.8 3.7 %all-to-all-start.2 = ((bf16[4,208,576]{2,0,1:T(4,128)(2,1)}), bf16[4,208,576]{2,0,1:T(4,128)(2,1)S(1)}, u32[]{:S(2)}, u32[]{:S(2)}) async-start(bf16[4,208,576]{2,0,1:T(4,128)(2,1)} %copy.96), calls=%async_computation.2 | async-start | bytes 2129920 | tf_op jit(solution)/shard_map/all_to_all | solution.py:375
  89.6 0.5 copy.89
  90.0 0.5 reshape.460
  90.5 0.7 copy.90
  91.2 1.1 copy.94.moved_ref
  92.2 18.7 %shard_map.155.temporal_ref = f32[208,1152]{1,0:T(8,128)} custom-call(bf16[4,208,424]{2,1,0:T(8,128)(2,1)} %copy.94.moved_ref, f32[208,2]{1,0:T(8,128)} %copy.95.closed_ref, bf16[512,512]{1,0:T(8,128)(2,1)} %constant.174.clone.perm_ref.inverse_ref, bf16[64,2048]{1,0:T(8,128)(2,1)} %constant.175.clone.spread_ref, ...), custom_call_target="tpu_custom_call" | custom-call | flops 20000000000 | bytes 8000000 | tf_op jit(solution)/shard_map/pallas_call | solution.py:267
  110.9 4.4 %all-to-all-done.2 = bf16[4,208,576]{2,0,1:T(4,128)(2,1)S(1)} async-done(((bf16[4,208,576]{2,0,1:T(4,128)(2,1)}), bf16[4,208,576]{2,0,1:T(4,128)(2,1)S(1)}, u32[]{:S(2)}, u32[]{:S(2)}) %all-to-all-start.2) | async-done | bytes 958496 | tf_op jit(solution)/shard_map/all_to_all | solution.py:375
  115.3 0.4 copy.97
  115.7 0.8 reshape.465
  116.5 0.4 copy.98
  116.9 1.1 copy.99.moved_ref
  118.0 5.6 %shard_map.157 = bf16[4,208,576]{2,1,0:T(8,128)(2,1)} custom-call(f32[208,1152]{1,0:T(8,128)} %shard_map.155.temporal_ref, bf16[4,208,576]{2,1,0:T(8,128)(2,1)} %copy.99.moved_ref, bf16[512,512]{1,0:T(8,128)(2,1)} %constant.174.clone.perm_ref.inverse_ref, bf16[512,512]{1,0:T(8,128)(2,1)} %constant.174.clone.perm_ref.inverse_ref, bf16[288,576]{1,0:T(8,128)(2,1)} %w_ref.1), custom_call_target="tpu_custom_call" | custom-call | flops 2000000000 | bytes 8000000 | tf_op jit(solution)/shard_map/pallas_call | solution.py:267
  123.6 1.6 %copy.100 = bf16[4,208,576]{2,0,1:T(4,128)(2,1)S(1)} copy(bf16[4,208,576]{2,1,0:T(8,128)(2,1)} %shard_map.157) | data formatting | bytes 1916928 | tf_op jit(solution)/shard_map/pallas_call | solution.py:267
  125.3 0.4 copy.101
  125.7 0.6 reshape.468
  126.4 0.3 reshape.469
  126.6 0.3 copy.102
  127.0 16.5 %all_to_all.47 = bf16[4,4,49,576]{3,1,2,0:T(4,128)(2,1)S(1)} all-to-all(bf16[4,4,49,576]{3,1,2,0:T(4,128)(2,1)S(1)} %copy.102), channel_id=1, replica_groups=mesh['groups'=2,'tm'=4,'space'=4] {'space'}, dimensions={0} | all-to-all | bytes 1806336 | tf_op jit(solution)/shard_map/all_to_all | solution.py:416
  143.5 0.7 reduce_sum.22
  144.2 1.0 reshape.470
  (72 shorter events, 2.0 us)
Async XLA Ops:
  0.0 3.1 %copy-start = (bf16[8,28224]{1,0:T(8,128)(2,1)S(1)}, bf16[8,28224]{1,0:T(8,128)(2,1)}, u32[]{:S(2)}) copy-start(bf16[8,28224]{1,0:T(8,128)(2,1)} %param.16) | copy-start | bytes 1354756
  3.1 1.0 copy-start.7
  4.2 11.7 %copy-start.8 = (s32[196,196]{1,0:T(8,128)S(1)}, s32[196,196]{1,0:T(8,128)}, u32[]{:S(2)}) copy-start(s32[196,196]{1,0:T(8,128)} %param.19) | copy-start | bytes 460996
  4.6 11.3 %copy-start.14 = (bf16[4,36,288]{2,0,1:T(4,128)(2,1)S(1)}, bf16[4,36,288]{2,0,1:T(4,128)(2,1)}, u32[]{:S(2)}) copy-start(bf16[4,36,288]{2,0,1:T(4,128)(2,1)} %param.23) | copy-start | bytes 248836
  4.6 23.1 %collective-permute-start = (bf16[288,272]{0,1:T(8,128)(2,1)S(1)}, bf16[288,272]{0,1:T(8,128)(2,1)S(1)}, u32[]{:S(2)}, u32[]{:S(2)}) collective-permute-start(bf16[288,272]{0,1:T(8,128)(2,1)S(1)} %concatenate.3), channel_id=1, source_target_pairs={{0,1},{1,2},{2,3},{3,0},{4,5},{5,6},{6,7},{7,4},{8,9},{9,10},{10,1... | collective-permute-start | bytes 470024 | tf_op jit(solution)/shard_map/ppermute | solution.py:330
  5.1 22.6 %collective-permute-start.1 = (bf16[288,272]{0,1:T(8,128)(2,1)S(1)}, bf16[288,272]{0,1:T(8,128)(2,1)S(1)}, u32[]{:S(2)}, u32[]{:S(2)}) collective-permute-start(bf16[288,272]{0,1:T(8,128)(2,1)S(1)} %concatenate.3), channel_id=1, source_target_pairs={{0,2},{1,3},{2,0},{3,1},{4,6},{5,7},{6,4},{7,5},{8,10},{9,11},{10,... | collective-permute-start | bytes 470024 | tf_op jit(solution)/shard_map/ppermute | solution.py:330
  7.7 20.0 %collective-permute-start.2 = (bf16[288,272]{0,1:T(8,128)(2,1)S(1)}, bf16[288,272]{0,1:T(8,128)(2,1)S(1)}, u32[]{:S(2)}, u32[]{:S(2)}) collective-permute-start(bf16[288,272]{0,1:T(8,128)(2,1)S(1)} %concatenate.3), channel_id=1, source_target_pairs={{0,3},{1,0},{2,1},{3,2},{4,7},{5,4},{6,5},{7,6},{8,11},{9,8},{10,9... | collective-permute-start | bytes 470024 | tf_op jit(solution)/shard_map/ppermute | solution.py:330
  10.1 21.4 %all-to-all-start = ((bf16[4,2,28224]{2,1,0:T(2,128)(2,1)}), bf16[4,2,28224]{2,1,0:T(2,128)(2,1)}, u32[]{:S(2)}, u32[]{:S(2)}) async-start(bf16[4,2,28224]{2,1,0:T(2,128)(2,1)} %all_to_all.33), calls=%async_computation | async-start | bytes 905216 | tf_op jit(solution)/shard_map/all_to_all | solution.py:320
  15.9 1.9 %copy-start.6 = (f32[288,1152]{1,0:T(8,128)S(1)}, f32[288,1152]{1,0:T(8,128)}, u32[]{:S(2)}) copy-start(f32[288,1152]{1,0:T(8,128)} %constant.173.clone) | copy-start | bytes 3981316
  15.9 1.9 %copy-start.9 = (f32[4,288,16]{1,2,0:T(8,128)S(1)}, f32[4,288,16]{1,2,0:T(8,128)}, u32[]{:S(2)}) copy-start(f32[4,288,16]{1,2,0:T(8,128)} %param.25) | copy-start | bytes 221188
  17.7 2.0 %copy-start.10 = (f32[4,288]{1,0:T(4,128)S(1)}, f32[4,288]{1,0:T(4,128)}, u32[]{:S(2)}) copy-start(f32[4,288]{1,0:T(4,128)} %param.24) | copy-start | bytes 13828
  19.0 1.6 %copy-start.11 = (f32[4,288]{1,0:T(4,128)S(1)}, f32[4,288]{1,0:T(4,128)}, u32[]{:S(2)}) copy-start(f32[4,288]{1,0:T(4,128)} %param.26) | copy-start | bytes 13828
  19.8 2.2 %copy-start.13 = (s32[4]{0:T(128)S(1)}, s32[4]{0:T(128)}, u32[]{:S(2)}) copy-start(s32[4]{0:T(128)} %param.18) | copy-start | bytes 52
  24.2 2.0 %copy-start.12 = (f32[576]{0:T(1024)S(1)}, f32[576]{0:T(1024)}, u32[]{:S(2)}) copy-start(f32[576]{0:T(1024)} %param.20) | copy-start | bytes 6916
  26.1 20.2 %copy-start.2 = (bf16[208,196]{1,0:T(8,128)(2,1)}, bf16[208,196]{1,0:T(8,128)(2,1)S(1)}, u32[]{:S(2)}) copy-start(bf16[208,196]{1,0:T(8,128)(2,1)S(1)} %reshape.459.pick_ref) | copy-start | bytes 244612
  46.4 1.8 %copy-start.1 = (bf16[2,576,1152]{2,1,0:T(8,128)(2,1)S(1)}, bf16[2,576,1152]{2,1,0:T(8,128)(2,1)}, u32[]{:S(2)}) copy-start(bf16[2,576,1152]{2,1,0:T(8,128)(2,1)} %all_ref.1) | copy-start | bytes 7962628
  54.7 0.8 copy-start.3
  55.6 0.8 copy-start.4
  56.4 0.8 copy-start.5
  58.7 27.1 %all-to-all-start.1 = ((bf16[4,208,424]{2,0,1:T(4,128)(2,1)}), bf16[4,208,424]{2,0,1:T(4,128)(2,1)S(1)}, u32[]{:S(2)}, u32[]{:S(2)}) async-start(bf16[4,208,424]{2,0,1:T(4,128)(2,1)} %copy.88), calls=%async_computation.1 | async-start | bytes 1703936 | tf_op jit(solution)/shard_map/all_to_all | solution.py:375
  85.8 29.5 %all-to-all-start.2 = ((bf16[4,208,576]{2,0,1:T(4,128)(2,1)}), bf16[4,208,576]{2,0,1:T(4,128)(2,1)S(1)}, u32[]{:S(2)}, u32[]{:S(2)}) async-start(bf16[4,208,576]{2,0,1:T(4,128)(2,1)} %copy.96), calls=%async_computation.2 | async-start | bytes 2129920 | tf_op jit(solution)/shard_map/all_to_all | solution.py:375
